TPU v7x, 512 devices: a whole 4x4x16 slice. The times are simulated.
512 devices in a mesh: dp: 8 (over y, core), seq: 16 (over z), tensor: 4 (over x).
Axes of the slice: x: 4, y: 4, z: 16, core: 2. Of those that a mesh axis runs over, the one named last changes fastest.
Arguments:
- queries: bfloat16 [8, 2048, 8192], P('dp', 'seq', 'tensor'), may hold values from -6 to 6
- keys: bfloat16 [8, 2048, 1024], P('dp', 'seq', 'tensor'), may hold values from -6 to 6
- output_gradient: bfloat16 [8, 2048, 8192], P('dp', 'seq', 'tensor'), may hold values from -6 to 6
- normed: bfloat16 [8, 2048, 4096], P('dp', 'seq', 'tensor'), may hold values from -6 to 6
- document_length: int32 [8, 8], P('dp'), may hold values from 1 to 1536, 2048 in all within a row
- codes: bfloat16 [4096, 1024], P(None, 'tensor'), may hold values from -8 to 7, as said below
- scales: float32 [32, 1024], P(None, 'tensor'), may hold values from 0.0015 to 0.006
- adapter_down: bfloat16 [4096, 64], P('tensor'), may hold values from -0.09375 to 0.09375
- adapter_up: bfloat16 [64, 1024], P(None, 'tensor'), may hold values from -0.75 to 0.75
Outputs:
- d_normed: bfloat16 [8, 2048, 4096], P('dp', 'seq', 'tensor')
- grad_a: float32 [4096, 64], P('tensor')
- grad_b: float32 [64, 1024], P(None, 'tensor')
Inputs may be any that keep to these rules, and one draw needn't show every extreme that they name: `codes`: whole-numbered levels.
All inputs are finite; a program needn't handle non-finite values.
Results may differ from a plain program's by a relative error of at most 0.02.
Values may be sent and summed in bfloat16 or wider, within the bound.
A program may use at most 64 MiB of HBM per device.

v0:
```python
import math

import jax
import jax.numpy as jnp
from jax import lax
from jax.sharding import PartitionSpec as P

MODEL_WIDTH = 4096
HEAD_SIZE = 128
GROUP_SIZE = 128


NEG = -1e30


def segment_ids(document_length, length):
    bounds = jnp.cumsum(document_length)
    positions = jnp.arange(length, dtype=jnp.int32)
    return jnp.sum((positions[:, None] >= bounds[None, :]).astype(jnp.int32), axis=1)


def head_values(query, key_rows, grad_rows, seg, block):
    length = key_rows.shape[0]
    positions = jnp.arange(length, dtype=jnp.int32)
    inverse = 1.0 / math.sqrt(query.shape[1])

    def step(total, index):
        first = index * block
        rows = lax.dynamic_slice_in_dim(query, first, block, 0)
        grads = lax.dynamic_slice_in_dim(grad_rows, first, block, 0)
        row_seg = lax.dynamic_slice_in_dim(seg, first, block, 0)
        row_pos = lax.dynamic_slice_in_dim(positions, first, block, 0)
        allowed = (row_seg[:, None] == seg[None, :]) & (positions[None, :] <= row_pos[:, None])
        scores = jnp.dot(rows, key_rows.T, preferred_element_type=jnp.float32) * inverse
        scores = jnp.where(allowed, scores, NEG)
        peak = jnp.max(scores, axis=1, keepdims=True)
        weights = jnp.where(allowed, jnp.exp(scores - peak), 0.0)
        probs = (weights / jnp.sum(weights, axis=1, keepdims=True)).astype(jnp.bfloat16)
        return (total + jnp.dot(probs.T, grads, preferred_element_type=jnp.float32), None)

    start = jnp.zeros((length, grad_rows.shape[1]), jnp.float32)
    total, unused = lax.scan(step, start, jnp.arange(length // block, dtype=jnp.int32))
    return total


def body(
    queries, keys, output_gradient, normed, document_length, codes, scales, adapter_down, adapter_up
):
    tok_rows = queries.shape[1]
    length = tok_rows * lax.axis_size("seq")
    heads_here = queries.shape[2] // HEAD_SIZE
    kv_here = keys.shape[2] // HEAD_SIZE
    group = heads_here // kv_here
    block = math.gcd(length, 512)
    seg = segment_ids(document_length[0], length)
    query_h = queries[0].reshape(tok_rows, heads_here, HEAD_SIZE)
    grad_h = output_gradient[0].reshape(tok_rows, heads_here, HEAD_SIZE)
    row_norm_inputs = normed[0]
    lowrank_piece = jnp.dot(row_norm_inputs, adapter_down, preferred_element_type=jnp.float32)
    lowrank_input = lax.psum(lowrank_piece.astype(jnp.bfloat16), "tensor").astype(jnp.float32)
    key_wide = jnp.repeat(keys[0].reshape(tok_rows, kv_here, HEAD_SIZE), group, axis=1)
    query_x, grad_x, key_x = (
        lax.all_to_all(query_h, "seq", split_axis=1, concat_axis=0, tiled=True),
        lax.all_to_all(grad_h, "seq", split_axis=1, concat_axis=0, tiled=True),
        lax.all_to_all(key_wide, "seq", split_axis=1, concat_axis=0, tiled=True),
    )

    def one_head(head):
        return head_values(query_x[:, head], key_x[:, head], grad_x[:, head], seg, block)

    each = lax.map(one_head, jnp.arange(query_x.shape[1], dtype=jnp.int32))
    returned = lax.all_to_all(
        jnp.transpose(each, (1, 0, 2)).astype(jnp.bfloat16),
        "seq",
        split_axis=0,
        concat_axis=1,
        tiled=True,
    ).astype(jnp.float32)
    value_gradient = (
        jnp.sum(returned.reshape(tok_rows, kv_here, group, HEAD_SIZE), axis=2)
        .reshape(tok_rows, kv_here * HEAD_SIZE)
        .astype(jnp.bfloat16)
    )
    gradient_piece = jnp.dot(value_gradient, adapter_up.T, preferred_element_type=jnp.float32)
    grad_low = lax.psum(gradient_piece.astype(jnp.bfloat16), "tensor")
    lowrank_input = lowrank_input.astype(jnp.bfloat16)
    cols = codes.shape[1]
    weight = (
        (
            codes.astype(jnp.float32).reshape(MODEL_WIDTH // GROUP_SIZE, GROUP_SIZE, cols)
            * scales[:, None, :]
        )
        .reshape(MODEL_WIDTH, cols)
        .astype(jnp.bfloat16)
    )
    base_term = jnp.dot(value_gradient, weight.T, preferred_element_type=jnp.float32)
    base = lax.psum_scatter(
        base_term.astype(jnp.bfloat16), "tensor", scatter_dimension=1, tiled=True
    ).astype(jnp.float32)
    adapter_branch = 2.0 * jnp.dot(grad_low, adapter_down.T, preferred_element_type=jnp.float32)
    d_normed = (base + adapter_branch).astype(jnp.bfloat16)[None]
    factor = 2.0 / math.sqrt(lax.axis_size("dp") * length)
    local_a = jnp.dot(row_norm_inputs.T, grad_low, preferred_element_type=jnp.float32) * factor
    local_b = jnp.dot(lowrank_input.T, value_gradient, preferred_element_type=jnp.float32) * factor
    grad_a, grad_b = lax.psum((local_a, local_b), ("dp", "seq"))
    return (d_normed, grad_a, grad_b)


def solution(mesh):
    placed = (
        P("dp", "seq", "tensor"),
        P("dp", "seq", "tensor"),
        P("dp", "seq", "tensor"),
        P("dp", "seq", "tensor"),
        P("dp", None),
        P(None, "tensor"),
        P(None, "tensor"),
        P("tensor", None),
        P(None, "tensor"),
    )
    return jax.shard_map(
        body,
        mesh=mesh,
        in_specs=placed,
        out_specs=(P("dp", "seq", "tensor"), P("tensor", None), P(None, "tensor")),
        check_vma=False,
    )
```

profile of v0, /device:TPU:1, one launch (start us, length us, event | category | flops | bytes accessed | tf_op | source)
XLA Modules:
  0.0 571.9 jit_solution(7335561158522034299)
XLA Ops:
  10.2 15.7 %all-to-all-start.2 = ((bf16[128,16,128]{2,0,1:T(8,128)(2,1)}), bf16[128,16,128]{2,0,1:T(8,128)(2,1)S(1)}, u32[]{:S(2)}, u32[]{:S(2)}) async-start(bf16[128,16,128]{2,0,1:T(8,128)(2,1)} %copy.25), calls=%async_computation.2 | async-start | bytes 1048576 | tf_op jit(solution)/shard_map/all_to_all | solution.py:64
  28.0 20.7 %all-to-all-done.2 = bf16[128,16,128]{2,0,1:T(8,128)(2,1)S(1)} async-done(((bf16[128,16,128]{2,0,1:T(8,128)(2,1)}), bf16[128,16,128]{2,0,1:T(8,128)(2,1)S(1)}, u32[]{:S(2)}, u32[]{:S(2)}) %all-to-all-start.2) | async-done | bytes 524320 | tf_op jit(solution)/shard_map/all_to_all | solution.py:64
  48.8 12.6 %all-to-all-start = ((bf16[128,16,128]{2,0,1:T(8,128)(2,1)}), bf16[128,16,128]{2,0,1:T(8,128)(2,1)S(1)}, u32[]{:S(2)}, u32[]{:S(2)}) async-start(bf16[128,16,128]{2,0,1:T(8,128)(2,1)} %copy.23), calls=%async_computation | async-start | bytes 1048576 | tf_op jit(solution)/shard_map/all_to_all | solution.py:63
  61.4 22.7 %all-to-all-done = bf16[128,16,128]{2,0,1:T(8,128)(2,1)S(1)} async-done(((bf16[128,16,128]{2,0,1:T(8,128)(2,1)}), bf16[128,16,128]{2,0,1:T(8,128)(2,1)S(1)}, u32[]{:S(2)}, u32[]{:S(2)}) %all-to-all-start) | async-done | bytes 524320 | tf_op jit(solution)/shard_map/all_to_all | solution.py:63
  85.0 12.6 %all-to-all-start.1 = ((bf16[128,16,128]{2,0,1:T(8,128)(2,1)}), bf16[128,16,128]{2,0,1:T(8,128)(2,1)S(1)}, u32[]{:S(2)}, u32[]{:S(2)}) async-start(bf16[128,16,128]{2,0,1:T(8,128)(2,1)} %bitcast.5), calls=%async_computation.1 | async-start | bytes 1048576 | tf_op jit(solution)/shard_map/all_to_all | solution.py:65
  98.0 22.5 %all-to-all-done.1 = bf16[128,16,128]{2,0,1:T(8,128)(2,1)S(1)} async-done(((bf16[128,16,128]{2,0,1:T(8,128)(2,1)}), bf16[128,16,128]{2,0,1:T(8,128)(2,1)S(1)}, u32[]{:S(2)}, u32[]{:S(2)}) %all-to-all-start.1) | async-done | bytes 524320 | tf_op jit(solution)/shard_map/all_to_all | solution.py:65
  120.5 42.4 %while.19 = (s32[]{:T(128)}, f32[2048,128]{1,0:T(8,128)S(1)}, s32[4]{0:T(128)S(1)}, s32[2048]{0:T(1024)S(1)}, s32[2048]{0:T(1024)S(1)}, /*index=5*/bf16[2048,128...) while((s32[]{:T(128)}, f32[2048,128]{1,0:T(8,128)S(1)}, ...), condition=%wide.region_5.6_spmd.clone.clone, body=%wide.region_2.0_spmd.clone.clone.sunk | while | flops 561511424 | bytes 32323812 | solution.py:42
  123.2 1.9 copy-done.1
  126.8 4.2 convolution_add_fusion.2
  133.8 1.9 copy-done.1
  137.4 4.2 convolution_add_fusion.2
  144.4 1.9 copy-done.1
  148.0 4.2 convolution_add_fusion.2
  155.0 1.9 copy-done.1
  158.6 4.2 convolution_add_fusion.2
  165.4 12.7 %all-to-all-start.3 = ((bf16[16,2,8192]{2,1,0:T(2,128)(2,1)}), bf16[16,2,8192]{2,1,0:T(2,128)(2,1)}, u32[]{:S(2)}, u32[]{:S(2)}) async-start(bf16[16,2,8192]{2,1,0:T(2,128)(2,1)} %reshape.61), calls=%async_computation.3 | async-start | bytes 1048576 | tf_op jit(solution)/shard_map/all_to_all | solution.py:72
  178.2 2.0 fusion.10
  180.2 20.8 %all-to-all-done.3 = bf16[16,2,8192]{2,1,0:T(2,128)(2,1)} async-done(((bf16[16,2,8192]{2,1,0:T(2,128)(2,1)}), bf16[16,2,8192]{2,1,0:T(2,128)(2,1)}, u32[]{:S(2)}, u32[]{:S(2)}) %all-to-all-start.3) | async-done | bytes 524320 | tf_op jit(solution)/shard_map/all_to_all | solution.py:72
  201.0 2.2 reshape.62
  205.3 1.8 convolution_convert_fusion
  207.6 13.4 %all-reduce.1 = (bf16[128,64]{0,1:T(8,128)(2,1)S(1)}, bf16[128,64]{0,1:T(8,128)(2,1)S(1)}) all-reduce(bf16[128,64]{0,1:T(8,128)(2,1)S(1)} %convolution_convert_fusion.1, bf16[128,64]{0,1:T(8,128)(2,1)S(1)} %convolution_convert_fusion.2), channel_id=1, replica_groups=mesh['dp'=8,'seq'=16,'tensor'=4] {'tensor'}, use_global_device_ids=true, to_apply=%region_8.9 | all-reduce | flops 16384 | bytes 65536 | tf_op jit(solution)/shard_map/psum | solution.py:85
  222.7 16.7 %reduce-scatter.2.cloned.1.call-done = bf16[128,1024]{1,0:T(8,128)(2,1)} async-done(((bf16[128,4096]{1,0:T(8,128)(2,1)}), bf16[128,1024]{1,0:T(8,128)(2,1)}) %reduce-scatter.2.cloned.1.call-update) | async-done | bytes 262160 | tf_op jit(solution)/shard_map/reduce_scatter | solution.py:97
  239.4 1.9 fusion.14
  241.3 320.0 %all-reduce.4.cloned.1.call-done = (f32[1024,64]{0,1:T(8,128)}, f32[64,256]{1,0:T(8,128)}) async-done(((f32[1024,64]{0,1:T(8,128)}, f32[64,256]{1,0:T(8,128)}), (f32[1024,64]{0,1:T(8,128)}, f32[64,256]{1,0:T(8,128)})) %all-reduce.4.cloned.1.call-update) | async-done | bytes 327696 | tf_op jit(solution)/shard_map/psum | solution.py:105
  (65 shorter events, 30.3 us)
Async XLA Ops:
  8.0 199.2 %copy-start = (bf16[1,128,1024]{2,1,0:T(8,128)(2,1)S(1)}, bf16[1,128,1024]{2,1,0:T(8,128)(2,1)}, u32[]{:S(2)}) copy-start(bf16[1,128,1024]{2,1,0:T(8,128)(2,1)} %param.14) | copy-start | bytes 786436
  8.0 53.3 %copy-start.3 = (bf16[1,128,256]{2,1,0:T(8,128)(2,1)S(1)}, bf16[1,128,256]{2,1,0:T(8,128)(2,1)}, u32[]{:S(2)}) copy-start(bf16[1,128,256]{2,1,0:T(8,128)(2,1)} %param.12) | copy-start | bytes 196612
  8.0 89.7 %copy-start.6 = (s32[1,8]{1,0:T(1,128)S(1)}, s32[1,8]{1,0:T(1,128)}, u32[]{:S(2)}) copy-start(s32[1,8]{1,0:T(1,128)} %param.15) | copy-start | bytes 100
  10.2 38.6 %all-to-all-start.2 = ((bf16[128,16,128]{2,0,1:T(8,128)(2,1)}), bf16[128,16,128]{2,0,1:T(8,128)(2,1)S(1)}, u32[]{:S(2)}, u32[]{:S(2)}) async-start(bf16[128,16,128]{2,0,1:T(8,128)(2,1)} %copy.25), calls=%async_computation.2 | async-start | bytes 1048576 | tf_op jit(solution)/shard_map/all_to_all | solution.py:64
  48.8 35.4 %all-to-all-start = ((bf16[128,16,128]{2,0,1:T(8,128)(2,1)}), bf16[128,16,128]{2,0,1:T(8,128)(2,1)S(1)}, u32[]{:S(2)}, u32[]{:S(2)}) async-start(bf16[128,16,128]{2,0,1:T(8,128)(2,1)} %copy.23), calls=%async_computation | async-start | bytes 1048576 | tf_op jit(solution)/shard_map/all_to_all | solution.py:63
  85.0 35.4 %all-to-all-start.1 = ((bf16[128,16,128]{2,0,1:T(8,128)(2,1)}), bf16[128,16,128]{2,0,1:T(8,128)(2,1)S(1)}, u32[]{:S(2)}, u32[]{:S(2)}) async-start(bf16[128,16,128]{2,0,1:T(8,128)(2,1)} %bitcast.5), calls=%async_computation.1 | async-start | bytes 1048576 | tf_op jit(solution)/shard_map/all_to_all | solution.py:65
  123.2 1.9 copy-start.1
  133.8 1.9 copy-start.1
  144.4 1.9 copy-start.1
  155.0 1.9 copy-start.1
  162.9 15.3 %copy-start.4 = (f32[32,256]{1,0:T(8,128)S(1)}, f32[32,256]{1,0:T(8,128)}, u32[]{:S(2)}) copy-start(f32[32,256]{1,0:T(8,128)} %param.17) | copy-start | bytes 98308
  165.4 35.6 %all-to-all-start.3 = ((bf16[16,2,8192]{2,1,0:T(2,128)(2,1)}), bf16[16,2,8192]{2,1,0:T(2,128)(2,1)}, u32[]{:S(2)}, u32[]{:S(2)}) async-start(bf16[16,2,8192]{2,1,0:T(2,128)(2,1)} %reshape.61), calls=%async_computation.3 | async-start | bytes 1048576 | tf_op jit(solution)/shard_map/all_to_all | solution.py:72
  178.1 61.3 %reduce-scatter.2.cloned.1.call-start = ((), (), s32[]{:S(2)}) async-start(), calls=%async_computation.5 | async-start | bytes 1310720 | tf_op jit(solution)/shard_map/reduce_scatter | solution.py:97
  180.2 27.0 %copy-start.2 = (bf16[1024,64]{0,1:T(8,128)(2,1)S(1)}, bf16[1024,64]{0,1:T(8,128)(2,1)}, u32[]{:S(2)}) copy-start(bf16[1024,64]{0,1:T(8,128)(2,1)} %param.18) | copy-start | bytes 393220
  204.1 3.4 copy-start.5
  207.2 354.1 %all-reduce.4.cloned.1.call-start = ((), (), s32[]{:S(2)}) async-start(), calls=%async_computation.6 | async-start | bytes 655360 | tf_op jit(solution)/shard_map/psum | solution.py:105
Sparse Core Ops, SparseCore 0:
  207.3 32.0 reduce-scatter.1
Sparse Core Ops, SparseCore 1:
  222.8 338.4 all-reduce.3
where the time goes:
time: 573 us; the launch traced here: 572 us
  waiting for transfers between devices  423 us (74%)
  starting transfers between devices  53.8 us (9%)
  matrix products  27.9 us (5%)
  local copies, waits for them, and re-layouts  23.6 us (4%)
  between operations  15.7 us (3%)
  blocking collectives  13.4 us (2%)
  other arithmetic  11.3 us (2%)
    psum x1, waiting for transfers between devices, body(): grad_a, grad_b = lax.psum((local_a, local_b), ('dp', 'seq'))  320 us
    all_to_all x1, waiting for transfers between devices, body(): lax.all_to_all(query_h, 'seq', split_axis=1, concat_axis=0, tiled=True)  22.7 us
    all_to_all x1, waiting for transfers between devices, body(): lax.all_to_all(key_wide, 'seq', split_axis=1, concat_axis=0, tiled=True)  22.5 us
    all_to_all x1, waiting for transfers between devices, body(): lax.all_to_all(jnp.transpose(each, (1, 0, 2)).astype(jnp.bfloat16), 'seq'...  20.8 us
    all_to_all x1, waiting for transfers between devices, body(): lax.all_to_all(grad_h, 'seq', split_axis=1, concat_axis=0, tiled=True)  20.7 us
    dot_general x4, matrix products, step(): jnp.dot(probs.T, grads, preferred_element_type=jnp.float32)  17 us
    reduce_scatter x1, waiting for transfers between devices, body(): lax.psum_scatter(base_term.astype(jnp.bfloat16), 'tensor', scatter_dimens...  16.7 us
    all_to_all x1, starting transfers between devices, body(): lax.all_to_all(grad_h, 'seq', split_axis=1, concat_axis=0, tiled=True)  15.7 us
  transfers between devices with their start and end apart: 6, of which 6 were waited for; matrix products, arithmetic and copies ran while one was open for 1% of the time, Pallas kernels for 0%

commit v1 on v0

v1 whole, which is shorter than its diff:
```python
import functools
import math

import jax
import jax.numpy as jnp
from jax import lax
from jax.experimental import pallas as pl
from jax.experimental.pallas import tpu as pltpu
from jax.sharding import PartitionSpec as P

MESH = pl.DeviceIdType.MESH
HEAD = 128
GROUP = 128
KV = 2
NEG = -1e30
F32 = jnp.float32
BF16 = jnp.bfloat16
NT = (((1,), (1,)), ((), ()))
TN = (((0,), (0,)), ((), ()))


def dot(a, b):
    return jnp.dot(a, b, preferred_element_type=F32)


def dot_general(a, b, dims):
    return lax.dot_general(a, b, dims, preferred_element_type=F32)


def kernel(
    shape,
    q_hbm, k_hbm, g_hbm, n_hbm, len_ref, codes_hbm, scales_hbm, down_hbm, up_hbm,
    dn_ref, ga_ref, gb_ref,
    kbuf, qv, qt, gv, nv, codes, scales, down, up, wst, wfull, bias_ref,
    m_ref, l_ref, ms_ref, w_ref, rs_l, rs_r, xa_buf, gx_buf, dv_buf,
    a_src, a_rcv, b_src, b_rcv, c_buf, d_buf,
    local_sem, f_send, f_recv, bk_send, bk_recv, ls, lr, rs, rr,
    w_send, w_recv, wc_send, wc_recv, xa_send, xa_recv, gx_send, gx_recv,
    dv_send, dv_recv, a_send, a_recv, b_send, b_recv, c_send, c_recv, d_send, d_recv,
):
    D, S, T = shape
    half = S // 2
    B = kbuf.shape[2]
    pairs = qt.shape[0]
    per_kv = pairs // KV
    feats = nv.shape[1]
    rank = up.shape[0]
    cols = up.shape[1]
    hf = feats // 2
    dp = lax.axis_index("dp")
    seq = lax.axis_index("seq")
    ten = lax.axis_index("tensor")
    core = lax.rem(dp, 2)
    sibling = dp + 1 - 2 * core
    right = {"seq": lax.rem(seq + 1, S)}
    left = {"seq": lax.rem(seq + S - 1, S)}

    def remote(src, dst, send, recv, where):
        return pltpu.make_async_remote_copy(
            src_ref=src, dst_ref=dst, send_sem=send, recv_sem=recv,
            device_id=where, device_id_type=MESH,
        )

    def local(src, dst, i):
        return pltpu.make_async_copy(src, dst, local_sem.at[i])

    in_k = [local(k_hbm.at[:, pl.ds(g * HEAD, HEAD)], kbuf.at[0, g], g) for g in range(KV)]
    in_q = local(q_hbm, qv, 2)
    in_codes = local(codes_hbm, codes, 3)
    in_scales = local(scales_hbm, scales, 4)
    in_n = local(n_hbm, nv, 5)
    in_down = local(down_hbm, down, 6)
    in_up = local(up_hbm, up, 7)
    in_g = [
        local(
            g_hbm.at[:, pl.ds(h * HEAD, HEAD)],
            gv.at[h // 2, pl.ds((h % 2) * B, B), :],
            8 + h,
        )
        for h in range(2 * pairs)
    ]
    for c in in_k + [in_q, in_codes, in_scales, in_n, in_down, in_up] + in_g:
        c.start()

    barrier = pltpu.get_barrier_semaphore()

    def greet(axis, me, size):
        def one(k, carry):
            pl.semaphore_signal(
                barrier, inc=1, device_id={axis: lax.rem(me + k, size)}, device_id_type=MESH
            )
            return carry
        lax.fori_loop(1, size, one, 0)

    greet("seq", seq, S)
    greet("tensor", ten, T)
    greet("dp", dp, D)
    for c in in_k:
        c.wait()
    pl.semaphore_wait(barrier, S + T + D - 3)

    def fwd(t, g):
        return remote(kbuf.at[t, g], kbuf.at[t + 1, g], f_send.at[t, g], f_recv.at[t + 1, g], right)

    def bwd(t, g):
        a = S - t if isinstance(t, int) and t == 0 else S - t
        src = kbuf.at[lax.rem(a, S), g]
        return remote(src, kbuf.at[S - 1 - t, g], bk_send.at[t, g], bk_recv.at[t + 1, g], left)

    fwd(0, 0).start()
    bwd(0, 1).start()
    fwd(0, 1).start()
    bwd(0, 0).start()

    ipos = seq * B + lax.broadcasted_iota(jnp.int32, (1, B), 1)
    start = jnp.zeros((1, B), jnp.int32)
    bound = jnp.int32(0)
    for d in range(len_ref.shape[1] - 1):
        bound = bound + len_ref[0, d]
        start = jnp.where(ipos >= bound, bound, start)
    jrow = lax.broadcasted_iota(jnp.int32, (B, B), 0)
    scale = math.log2(math.e) / math.sqrt(HEAD)

    in_q.wait()
    for h in range(2 * pairs):
        qt[h // 2, :, (h % 2) * B : (h % 2 + 1) * B] = qv[:, h * HEAD : (h + 1) * HEAD].T
    m_ref[...] = jnp.full(m_ref.shape, NEG, F32)
    l_ref[...] = jnp.zeros(l_ref.shape, F32)

    def attend(slots, t):
        for n, slot in enumerate(slots):
            jpos = lax.rem(seq - slot + S, S) * B + jrow
            allowed = (jpos >= start) & (jpos <= ipos)
            bias_ref[n] = jnp.where(allowed, 0.0, NEG).astype(F32)

        def pair(hp, carry):
            g = lax.div(hp, per_kv)
            wide = qt[hp]
            ts = []
            for n, slot in enumerate(slots):
                b = bias_ref[n]
                ts.append(dot(kbuf[slot, g], wide) * scale + jnp.concatenate([b, b], axis=1))
            peak = ts[0] if len(ts) == 1 else jnp.maximum(ts[0], ts[1])
            old = m_ref[hp]
            new = jnp.maximum(old, jnp.max(peak, axis=0, keepdims=True))
            total = l_ref[hp] * jnp.exp2(old - new)
            ws = [jnp.exp2(x - new) for x in ts]
            both = ws[0] if len(ws) == 1 else ws[0] + ws[1]
            l_ref[hp] = total + jnp.sum(both, axis=0, keepdims=True)
            for w, slot in zip(ws, slots):
                w_ref[slot, hp] = w.astype(BF16)
            m_ref[hp] = new
            ms_ref[t, hp] = new
            return carry

        lax.fori_loop(0, pairs, pair, 0)

    attend([0], 0)

    in_n.wait()
    in_down.wait()
    xa_buf[0] = dot_general(down[...], nv[...], NT).astype(BF16)

    def xa_copy(k):
        return remote(
            xa_buf.at[0], xa_buf.at[k], xa_send.at[k], xa_recv.at[k], {"tensor": lax.rem(ten + k, T)}
        )

    for k in range(1, T):
        xa_copy(k).start()

    in_codes.wait()
    in_scales.wait()

    def dequantised(first, n, put):
        def one(i, carry):
            row = pl.multiple_of(first + i * GROUP, GROUP)
            block = codes[pl.ds(row, GROUP), :].astype(F32)
            put(i, (block * scales[pl.ds(lax.div(row, GROUP), 1), :]).astype(BF16))
            return carry
        lax.fori_loop(0, n // GROUP, one, 0)

    def w_copy(k):
        return remote(
            wst.at[k], wfull.at[k, core], w_send.at[k], w_recv.at[k], {"tensor": lax.rem(ten + k, T)}
        )

    def wc_copy(k, h):
        return remote(wfull.at[k, h], wfull.at[k, h], wc_send.at[k], wc_recv.at[k], {"dp": sibling})

    for k in range(1, T):
        def put(i, value, k=k):
            wst[k, pl.ds(pl.multiple_of(i * GROUP, GROUP), GROUP), :] = value
        dequantised(lax.rem(ten + k, T) * feats + core * hf, hf, put)
        w_copy(k).start()
    for h in range(2):
        def put(i, value, h=h):
            wfull[0, h, pl.ds(pl.multiple_of(i * GROUP, GROUP), GROUP), :] = value
        dequantised(ten * feats + h * hf, hf, put)

    def pass_on(t, f1, b0):
        fwd(t - 1, 0).wait_recv()
        fwd(t, 0).start()
        bwd(t - 1, 1).wait_recv()
        bwd(t, 1).start()
        fwd(t - 1, 1).wait_recv()
        if f1:
            fwd(t, 1).start()
        bwd(t - 1, 0).wait_recv()
        if b0:
            bwd(t, 0).start()

    def ring(t, carry):
        pass_on(t, True, True)
        attend([t, S - t], t)
        return carry

    lax.fori_loop(1, half - 1, ring, 0)
    pass_on(half - 1, False, False)
    attend([half - 1, half + 1], half - 1)
    fwd(half - 1, 0).wait_recv()
    bwd(half - 1, 1).wait_recv()
    attend([half], half)

    l_ref[...] = 1.0 / l_ref[...]
    for c in in_g:
        c.wait()

    def partial(slot, t, g):
        total = None
        for i in range(per_kv):
            hp = g * per_kv + i
            factor = jnp.exp2(ms_ref[t, hp] - m_ref[hp]) * l_ref[hp]
            p = (w_ref[slot, hp].astype(F32) * factor).astype(BF16)
            one = dot(p, gv[hp])
            total = one if total is None else total + one
        return total

    def go_l(u, g):
        return remote(rs_l.at[u, g], rs_l.at[u + 1, g], ls.at[u, g], lr.at[u + 1, g], left)

    def go_r(u, g):
        return remote(rs_r.at[u, g], rs_r.at[u + 1, g], rs.at[u, g], rr.at[u + 1, g], right)

    rs_l[0, 0] = partial(half, half, 0).astype(BF16)
    go_l(0, 0).start()
    rs_r[0, 1] = partial(half, half, 1).astype(BF16)
    go_r(0, 1).start()

    def reduce_step(u, first):
        a, b, t = half - u, half + u, half - u
        al = [partial(a, t, g) for g in range(KV)]
        br = [partial(b, t, g) for g in range(KV)]
        go_l(u - 1, 0).wait_recv()
        rs_l[u, 0] = (al[0] + rs_l[u, 0].astype(F32)).astype(BF16)
        go_l(u, 0).start()
        go_r(u - 1, 1).wait_recv()
        rs_r[u, 1] = (br[1] + rs_r[u, 1].astype(F32)).astype(BF16)
        go_r(u, 1).start()
        if first:
            rs_l[u, 1] = al[1].astype(BF16)
        else:
            go_l(u - 1, 1).wait_recv()
            rs_l[u, 1] = (al[1] + rs_l[u, 1].astype(F32)).astype(BF16)
        go_l(u, 1).start()
        if first:
            rs_r[u, 0] = br[0].astype(BF16)
        else:
            go_r(u - 1, 0).wait_recv()
            rs_r[u, 0] = (br[0] + rs_r[u, 0].astype(F32)).astype(BF16)
        go_r(u, 0).start()

    reduce_step(1, True)

    def reduce_loop(u, carry):
        reduce_step(u, False)
        return carry

    lax.fori_loop(2, half, reduce_loop, 0)

    own = [partial(0, 0, g) for g in range(KV)]
    for k in range(1, T):
        xa_copy(k).wait_recv()
    xat = xa_buf[0].astype(F32)
    for k in range(1, T):
        xat = xat + xa_buf[k].astype(F32)
    xat = xat.astype(BF16)
    for k in range(1, T):
        w_copy(k).wait_recv()
        wc_copy(k, core).start()
    in_up.wait()
    for g in range(KV):
        go_l(half - 1, g).wait_recv()
        go_r(half - 1, g).wait_recv()
        dv_buf[0, :, g * HEAD : (g + 1) * HEAD] = (
            own[g] + rs_l[half, g].astype(F32) + rs_r[half, g].astype(F32)
        ).astype(BF16)

    dv = dv_buf[0]
    gx_buf[0] = dot_general(up[...], dv, NT).astype(BF16)

    def gx_copy(k):
        return remote(
            gx_buf.at[0], gx_buf.at[k], gx_send.at[k], gx_recv.at[k], {"tensor": lax.rem(ten + k, T)}
        )

    def dv_copy(k):
        return remote(
            dv_buf.at[0], dv_buf.at[k], dv_send.at[k], dv_recv.at[k], {"tensor": lax.rem(ten + k, T)}
        )

    for k in range(1, T):
        gx_copy(k).start()
    for k in range(1, T):
        dv_copy(k).start()
    per = a_src.shape[1]
    across = (feats + cols) // 128

    def tile_at(i, j):
        n = i * across + j
        return n // per, n % per

    part_b = dot(xat, dv)
    for i in range(rank // 16):
        for j in range(cols // 128):
            p, q = tile_at(i, feats // 128 + j)
            a_src[p, q] = part_b[i * 16 : i * 16 + 16, j * 128 : j * 128 + 128].astype(BF16)
    for k in range(1, T):
        gx_copy(k).wait_recv()
    gpt = gx_buf[0].astype(F32)
    for k in range(1, T):
        gpt = gpt + gx_buf[k].astype(F32)
    gpt = gpt.astype(BF16)
    for j in range(feats // 128):
        part_a = dot(gpt, nv[:, j * 128 : j * 128 + 128])
        for i in range(rank // 16):
            p, q = tile_at(i, j)
            a_src[p, q] = part_a[i * 16 : i * 16 + 16].astype(BF16)

    def a_copy(k):
        peer = lax.rem(dp + k, D)
        return remote(a_src.at[peer], a_rcv.at[k], a_send.at[k], a_recv.at[k], {"dp": peer})

    for k in range(1, D):
        a_copy(k).start()
    for k in range(1, D):
        a_copy(k).wait_recv()
    total = a_src[dp].astype(F32)
    for k in range(1, D):
        total = total + a_rcv[k].astype(F32)
    b_src[...] = total.astype(BF16)

    owners = [j * S // per for j in range(per)]

    def b_copy(j):
        away = lax.rem(owners[j] - seq + S, S)
        return remote(
            b_src.at[j], b_rcv.at[away], b_send.at[j], b_recv.at[away], {"seq": jnp.int32(owners[j])}
        )

    mine = jnp.int32(0)
    owner = seq == owners[0]
    for j in range(1, per):
        mine = jnp.where(seq == owners[j], j, mine)
        owner = owner | (seq == owners[j])

    for j in range(per):
        @pl.when(seq != owners[j])
        def _():
            b_copy(j).start()

    def c_copy(k):
        return remote(
            c_buf.at[mine], c_buf.at[mine], c_send.at[k], c_recv.at[mine], {"seq": lax.rem(seq + k, S)}
        )

    @pl.when(owner)
    def _():
        total = b_src[mine].astype(F32)
        for k in range(1, S):
            remote(
                b_src.at[0], b_rcv.at[k], b_send.at[0], b_recv.at[k], {"seq": lax.rem(seq + k, S)}
            ).wait_recv()
            total = total + b_rcv[k].astype(F32)
        c_buf[mine] = total.astype(BF16)
        for k in range(1, S):
            c_copy(k).start()

    for j in range(per):
        @pl.when(seq != owners[j])
        def _():
            remote(
                b_src.at[j], c_buf.at[j], c_send.at[0], c_recv.at[j], {"seq": jnp.int32(owners[j])}
            ).wait_recv()

    def d_copy(k):
        return remote(
            c_buf, d_buf.at[dp], d_send.at[k], d_recv.at[dp], {"dp": lax.rem(dp + k, D)}
        )

    for k in range(1, D):
        d_copy(k).start()
    d_buf[dp] = c_buf[...]

    gp = gpt.T
    for k in range(1, T):
        dv_copy(k).wait_recv()
        wc_copy(k, 1 - core).wait_recv()
    width = min(256, hf)
    for n in range(feats // width):
        h, row = n * width // hf, n * width % hf
        at = slice(n * width, (n + 1) * width)
        total = 2.0 * dot(gp, down[:, at])
        for k in range(T):
            total = total + dot_general(dv_buf[k], wfull[k, h, row : row + width, :], NT)
        dn_ref[:, at] = total.astype(BF16)

    for k in range(1, D):
        peer = lax.rem(dp + k, D)
        remote(c_buf, d_buf.at[peer], d_send.at[k], d_recv.at[peer], {"dp": peer}).wait_recv()
    factor = 2.0 / math.sqrt(D * S * B)
    for i in range(rank // 16):
        for j in range(across):
            p, q = tile_at(i, j)
            value = d_buf[p, q].astype(F32) * factor
            if j < feats // 128:
                ga_ref[i * 16 : i * 16 + 16, j * 128 : j * 128 + 128] = value
            else:
                c = j * 128 - feats
                gb_ref[i * 16 : i * 16 + 16, c : c + 128] = value

    for t in range(half):
        fwd(t, 0).wait_send()
        bwd(t, 1).wait_send()
        go_l(t, 0).wait_send()
        go_r(t, 1).wait_send()
        if t < half - 1:
            fwd(t, 1).wait_send()
            bwd(t, 0).wait_send()
        if t > 0:
            go_l(t, 1).wait_send()
            go_r(t, 0).wait_send()
    for k in range(1, T):
        xa_copy(k).wait_send()
        w_copy(k).wait_send()
        wc_copy(k, core).wait_send()
        gx_copy(k).wait_send()
        dv_copy(k).wait_send()
    for k in range(1, D):
        a_copy(k).wait_send()
        d_copy(k).wait_send()
    for j in range(per):
        @pl.when(seq != owners[j])
        def _():
            b_copy(j).wait_send()

    @pl.when(owner)
    def _():
        for k in range(1, S):
            c_copy(k).wait_send()


def body(
    shape, queries, keys, output_gradient, normed, document_length, codes, scales,
    adapter_down, adapter_up,
):
    D, S, T = shape
    B = queries.shape[1]
    heads = queries.shape[2] // HEAD
    pairs = heads // 2
    feats = normed.shape[2]
    rank, cols = adapter_up.shape
    half = S // 2
    per = (rank // 16) * ((feats + cols) // 128) // D
    anyspace = pl.BlockSpec(memory_space=pl.ANY)
    vmem = pl.BlockSpec(memory_space=pltpu.VMEM)
    smem = pl.BlockSpec(memory_space=pltpu.SMEM)
    dma = pltpu.SemaphoreType.DMA
    d_normed, grad_a, grad_b = pl.pallas_call(
        functools.partial(kernel, shape),
        out_shape=(
            jax.ShapeDtypeStruct((B, feats), BF16),
            jax.ShapeDtypeStruct((rank, feats), F32),
            jax.ShapeDtypeStruct((rank, cols), F32),
        ),
        in_specs=[anyspace] * 4 + [smem] + [anyspace] * 4,
        out_specs=(vmem, vmem, vmem),
        scratch_shapes=[
            pltpu.VMEM((S, KV, B, HEAD), BF16),
            pltpu.VMEM((B, heads * HEAD), BF16),
            pltpu.VMEM((pairs, HEAD, 2 * B), BF16),
            pltpu.VMEM((pairs, 2 * B, HEAD), BF16),
            pltpu.VMEM((B, feats), BF16),
            pltpu.VMEM(codes.shape, BF16),
            pltpu.VMEM(scales.shape, F32),
            pltpu.VMEM((rank, feats), BF16),
            pltpu.VMEM((rank, cols), BF16),
            pltpu.VMEM((T, feats // 2, cols), BF16),
            pltpu.VMEM((T, 2, feats // 2, cols), BF16),
            pltpu.VMEM((2, B, B), F32),
            pltpu.VMEM((pairs, 1, 2 * B), F32),
            pltpu.VMEM((pairs, 1, 2 * B), F32),
            pltpu.VMEM((half + 1, pairs, 1, 2 * B), F32),
            pltpu.VMEM((S, pairs, B, 2 * B), BF16),
            pltpu.VMEM((half + 1, KV, B, HEAD), BF16),
            pltpu.VMEM((half + 1, KV, B, HEAD), BF16),
            pltpu.VMEM((T, rank, B), BF16),
            pltpu.VMEM((T, rank, B), BF16),
            pltpu.VMEM((T, B, cols), BF16),
            pltpu.VMEM((D, per, 16, 128), BF16),
            pltpu.VMEM((D, per, 16, 128), BF16),
            pltpu.VMEM((per, 16, 128), BF16),
            pltpu.VMEM((S, 16, 128), BF16),
            pltpu.VMEM((per, 16, 128), BF16),
            pltpu.VMEM((D, per, 16, 128), BF16),
            dma((8 + heads,)),
            dma((half + 1, KV)),
            dma((half + 1, KV)),
            dma((half + 1, KV)),
            dma((half + 1, KV)),
            dma((half + 1, KV)),
            dma((half + 1, KV)),
            dma((half + 1, KV)),
            dma((half + 1, KV)),
            dma((T,)),
            dma((T,)),
            dma((T,)),
            dma((T,)),
            dma((T,)),
            dma((T,)),
            dma((T,)),
            dma((T,)),
            dma((T,)),
            dma((T,)),
            dma((D,)),
            dma((D,)),
            dma((per,)),
            dma((S,)),
            dma((S,)),
            dma((per,)),
            dma((D,)),
            dma((D,)),
        ],
        compiler_params=pltpu.CompilerParams(
            collective_id=0, has_side_effects=True, vmem_limit_bytes=40 * 1024 * 1024
        ),
        name="value_backward",
    )(
        queries[0], keys[0], output_gradient[0], normed[0], document_length, codes, scales,
        adapter_down.T, adapter_up,
    )
    return d_normed[None], grad_a.T, grad_b


def solution(mesh):
    shape = tuple(mesh.shape[a] for a in ("dp", "seq", "tensor"))
    split = P("dp", "seq", "tensor")
    placed = (
        split, split, split, split,
        P("dp", None), P(None, "tensor"), P(None, "tensor"), P("tensor", None), P(None, "tensor"),
    )
    return jax.shard_map(
        functools.partial(body, shape),
        mesh=mesh,
        in_specs=placed,
        out_specs=(split, P("tensor", None), P(None, "tensor")),
        check_vma=False,
    )
```

time: 573 us -> 114 us (0.20)
  waiting for transfers between devices: 423 us -> 0 us
  Pallas kernels: 0 us -> 102 us
  starting transfers between devices: 53.8 us -> 0 us
  matrix products: 27.9 us -> 0 us
  between operations: 15.7 us -> 0.66 us
  blocking collectives: 13.4 us -> 0 us
  local copies, waits for them, and re-layouts: 23.6 us -> 10.6 us
  other arithmetic: 11.3 us -> 0 us
    psum x1 -> x0, waiting for transfers between devices: 320 us -> none  [body(): grad_a, grad_b = lax.psum((local_a, local_b), ('dp', 'seq'))]
    pallas_call x0 -> x1, Pallas kernels: none -> 102 us  [body(): pl.pallas_call(functools.partial(kernel, shape), out_shape=(jax.ShapeDtyp...]
    all_to_all x4 -> x0, waiting for transfers between devices: 86.8 us -> none  [the longest x1 22.7 us: body(): lax.all_to_all(query_h, 'seq', split_axis=1, concat_axis=0, tiled=True)]
    all_to_all x4 -> x0, starting transfers between devices: 53.7 us -> none  [the longest x1 15.7 us: body(): lax.all_to_all(grad_h, 'seq', split_axis=1, concat_axis=0, tiled=True)]
    dot_general x14 -> x0, matrix products: 27.9 us -> none  [the longest x4 17 us: step(): jnp.dot(probs.T, grads, preferred_element_type=jnp.float32)]
    reduce_scatter x1 -> x0, waiting for transfers between devices: 16.7 us -> none  [body(): lax.psum_scatter(base_term.astype(jnp.bfloat16), 'tensor', scatter_dimens...]
    psum x1 -> x0, blocking collectives: 13.4 us -> none  [body(): grad_low = lax.psum(gradient_piece.astype(jnp.bfloat16), 'tensor')]
    reduce_sum x6 -> x0, other arithmetic: 8 us -> none  [the longest x4 6.79 us: step(): jnp.sum(weights, axis=1, keepdims=True)]
  transfers between devices with their start and end apart: 6 -> 0, of which waited for: 6 -> 0; matrix products, arithmetic and copies ran while one was open for 1% -> 0% of each run, Pallas kernels for 0% -> 0%
where the time goes in v1:
time: 114 us
  Pallas kernels  102 us (89%)
  local copies, waits for them, and re-layouts  10.6 us (9%)
    pallas_call x1, Pallas kernels, body(): pl.pallas_call(functools.partial(kernel, shape), out_shape=(jax.ShapeDtyp...  102 us
    unnamed x21, local copies, waits for them, and re-layouts  10.6 us

profile of v1, /device:TPU:1, one launch (start us, length us, event | category | flops | bytes accessed | tf_op | source)
XLA Modules:
  0.0 113.6 jit_solution(10035984322962747880)
XLA Ops:
  0.6 0.0 copy-start
  0.6 1.6 %copy-done = bf16[4096,256]{1,0:T(8,128)(2,1)S(1)} copy-done((bf16[4096,256]{1,0:T(8,128)(2,1)S(1)}, bf16[4096,256]{1,0:T(8,128)(2,1)}, u32[]{:S(2)}) %copy-start) | copy-done | bytes 2097176
  2.2 0.0 copy-start.1
  2.2 1.0 copy-done.1
  3.3 0.0 copy-start.2
  3.3 1.0 copy-done.2
  4.3 0.0 copy-start.3
  4.3 0.9 copy-done.3
  5.3 0.0 copy-start.4
  5.3 0.9 copy-done.4
  6.2 0.0 copy-start.5
  6.2 0.8 copy-done.5
  7.0 0.0 copy-start.6
  7.0 0.8 copy-done.6
  7.8 0.0 copy-start.7
  7.8 0.8 copy-done.7
  8.5 0.0 copy-start.8
  8.5 0.7 copy-done.8
  9.2 102.4 %value_backward.1 = (bf16[128,1024]{1,0:T(8,128)(2,1)S(1)}, f32[64,1024]{1,0:T(8,128)S(1)}, f32[64,256]{1,0:T(8,128)S(1)}) custom-call(bf16[128,2048]{1,0:T(8,128)(2,1)S(1)} %bitcast.7, bf16[128,256]{1,0:T(8,128)(2,1)S(1)} %bitcast.13, bf16[128,2048]{1,0:T(8,128)(2,1)S(1)} %bitcast.8, bf16[128,1024]{1,0:T(8,128)(2,1)S(1)} %bitcast.11, s32[1,8]{1,0:T(1,128)S(1)} %copy-done.8, ...), custom_call_target="tpu_custom_call" | custom-call | tf_op jit(solution)/shard_map/value_backward/pallas_call | solution.py:479
  111.6 0.7 copy.15
  112.3 0.7 copy.16
  113.0 0.6 copy.17
Async XLA Ops:
  0.6 1.6 %copy-start = (bf16[4096,256]{1,0:T(8,128)(2,1)S(1)}, bf16[4096,256]{1,0:T(8,128)(2,1)}, u32[]{:S(2)}) copy-start(bf16[4096,256]{1,0:T(8,128)(2,1)} %codes_hbm.1) | copy-start | bytes 6291460
  2.2 1.0 copy-start.1
  3.3 1.0 copy-start.2
  4.3 0.9 copy-start.3
  5.3 0.9 copy-start.4
  6.2 0.8 copy-start.5
  7.0 0.8 copy-start.6
  7.8 0.8 copy-start.7
  8.5 0.7 copy-start.8

commit v2 on v1

v2 whole, which is shorter than its diff:
```python
import functools
import math

import jax
import jax.numpy as jnp
from jax import lax
from jax.experimental import pallas as pl
from jax.experimental.pallas import tpu as pltpu
from jax.sharding import PartitionSpec as P

MESH = pl.DeviceIdType.MESH
HEAD = 128
GROUP = 128
KV = 2
NEG = -1e30
F32 = jnp.float32
BF16 = jnp.bfloat16
NT = (((1,), (1,)), ((), ()))
TN = (((0,), (0,)), ((), ()))


def dot(a, b):
    return jnp.dot(a, b, preferred_element_type=F32)


def dot_general(a, b, dims):
    return lax.dot_general(a, b, dims, preferred_element_type=F32)


class Tree:
    def __init__(self, size):
        half, last = size // 2, size - 1
        if size == 16:
            self.parent = {3: 0, 1: 0, 6: 3, 2: 3, 8: 6, 4: 6, 7: 6, 5: 6}
            self.after = {3: [1], 6: [2]}
            self.far_relays = {3: [15], 6: [12]}
            self.final = [7, 5, 8, 4]
            self.far_planes = [15, 12]
            self.far_leaves = [14, 13, 11, 10, 9]
        else:
            self.parent = {2: 0, 1: 2}
            self.after = {2: []}
            self.far_relays = {2: [last]}
            self.final = [1]
            self.far_planes = [last]
            self.far_leaves = []
        self.relays = list(self.after)
        self.children = {a: [b for b in self.parent if self.parent[b] == a] for a in range(half + 1)}
        self.least = {b: min(self.below(b)) for b in self.parent}
        self.wrapped = list(range(half - 1))
        self.last = last
        self.half = half
        self.far_index = {}
        for a in range(size):
            edges = [(b, c) for c in self.wrapped for (x, b) in self.far_edges(c) if x == a]
            for e, (b, c) in enumerate(edges):
                self.far_index[a, b, c] = e
        self.far_most = max(self.far_index.values()) + 1

    def below(self, b):
        return [b] + [x for child in self.children[b] for x in self.below(child)]

    def far_parent(self, plane, c):
        if plane - c <= self.half:
            return None
        if plane == self.last:
            return c
        if plane in (14, 12) or (plane, c) == (13, 4):
            return 15
        return 12

    def far_edges(self, c):
        return [(self.far_parent(b, c), b) for b in range(c + self.half + 1, self.last + 1)]

    def far_children(self, plane, c):
        return [b for a, b in self.far_edges(c) if a == plane]


def kernel(
    shape,
    q_hbm, k_hbm, g_hbm, n_hbm, len_hbm, codes_hbm, scales_hbm, down_hbm, up_hbm,
    dn_ref, ga_ref, gb_ref,
    len_ref, kbuf, qv, qt, gv, nv, codes, scales, down, up, wst, wfull, bias_ref,
    m_ref, l_ref, ms_ref, w_ref, acc_ref, rs_out, rs_in, rs_far, xa_buf, gx_buf, dv_buf,
    a_src, a_rcv, b_src, b_rcv, c_buf, d_buf,
    local_sem, k_send, k_recv, s_send, s_recv, far_recv,
    w_send, w_recv, wc_send, wc_recv, xa_send, xa_recv, gx_send, gx_recv,
    dv_send, dv_recv, a_send, a_recv, b_send, b_recv, c_send, c_recv, d_send, d_recv,
):
    D, S, T = shape
    half = S // 2
    tree = Tree(S)
    B = kbuf.shape[2]
    pairs = qt.shape[0]
    per_kv = pairs // KV
    feats = nv.shape[1]
    rank = up.shape[0]
    cols = up.shape[1]
    hf = feats // 2
    dp = lax.axis_index("dp")
    seq = lax.axis_index("seq")
    ten = lax.axis_index("tensor")
    core = lax.rem(dp, 2)
    sibling = dp + 1 - 2 * core
    near = min(3, half)
    last = S - 1

    def remote(src, dst, send, recv, where):
        return pltpu.make_async_remote_copy(
            src_ref=src, dst_ref=dst, send_sem=send, recv_sem=recv,
            device_id=where, device_id_type=MESH,
        )

    def local(src, dst, i):
        return pltpu.make_async_copy(src, dst, local_sem.at[i])

    in_k = [local(k_hbm.at[:, pl.ds(g * HEAD, HEAD)], kbuf.at[0, g], g) for g in range(KV)]
    in_q = local(q_hbm, qv, 2)
    in_codes = local(codes_hbm, codes, 3)
    in_scales = local(scales_hbm, scales, 4)
    in_n = local(n_hbm, nv, 5)
    in_down = local(down_hbm, down, 6)
    in_up = local(up_hbm, up, 7)
    in_len = local(len_hbm, len_ref, 8)
    in_g = [
        local(
            g_hbm.at[:, pl.ds(h * HEAD, HEAD)],
            gv.at[h // 2, pl.ds((h % 2) * B, B), :],
            9 + h,
        )
        for h in range(2 * pairs)
    ]
    due = {"k": in_k, "q": [in_q, in_len], "n": [in_n, in_down], "w": [in_codes, in_scales]}
    due.update({"g": in_g, "up": [in_up]})
    for group in ("k", "q", "n", "w", "g", "up"):
        for c in due[group]:
            c.start()

    def ready(group):
        for c in due.pop(group):
            c.wait()

    sent = []
    coming = {}

    def send(copies, group=None):
        for c in copies:
            c.start()
        sent.extend(copies)
        if group:
            coming[group] = copies

    def arrive(group):
        for c in coming.pop(group):
            c.wait_recv()

    barrier = pltpu.get_barrier_semaphore()

    def greet(axis, me, size):
        def one(k, carry):
            pl.semaphore_signal(
                barrier, inc=1, device_id={axis: lax.rem(me + k, size)}, device_id_type=MESH
            )
            return carry
        lax.fori_loop(1, size, one, 0)

    for k in range(1, near + 1):
        for away in (k, S - k):
            pl.semaphore_signal(
                barrier, inc=1, device_id={"seq": lax.rem(seq + away, S)}, device_id_type=MESH
            )
    greet("tensor", ten, T)
    greet("dp", dp, D)
    remotes = [c for c in tree.wrapped if near <= c < last - near]
    if remotes:
        @pl.when(seq == last)
        def _():
            for c in remotes:
                pl.semaphore_signal(
                    barrier, inc=1, device_id={"seq": jnp.int32(c)}, device_id_type=MESH
                )

    def k_copy(a, b, where):
        return remote(kbuf.at[a], kbuf.at[b], k_send.at[b], k_recv.at[b], {"seq": where})

    def runs(b):
        return lax.rem(seq - b + S, S) + tree.least[b] <= last

    def pass_down(a):
        for b in tree.children[a]:
            @pl.when(lax.rem(seq - a + S, S) + tree.least[b] <= last)
            def _(b=b):
                k_copy(a, b, lax.rem(seq + b - a + S, S)).start()

    def k_arrive(b):
        k_copy(0, b, seq).wait_recv()

    def far_copy(c, a, b):
        here, there = a - c, b - c
        return remote(
            kbuf.at[here], kbuf.at[there], k_send.at[S + tree.far_index[a, b, c]], k_recv.at[there],
            {"seq": jnp.int32(b)},
        )

    def pass_far(a):
        for c in tree.wrapped:
            if tree.far_parent(a, c) is None:
                continue
            k_arrive(a - c)
            for b in tree.far_children(a, c):
                far_copy(c, a, b).start()

    ready("q")
    ready("k")
    ipos = seq * B + lax.broadcasted_iota(jnp.int32, (1, B), 1)
    start = jnp.zeros((1, B), jnp.int32)
    bound = jnp.int32(0)
    for d in range(len_ref.shape[1] - 1):
        bound = bound + len_ref[0, d]
        start = jnp.where(ipos >= bound, bound, start)
    jrow = lax.broadcasted_iota(jnp.int32, (B, B), 0)
    scale = math.log2(math.e) / math.sqrt(HEAD)

    for h in range(2 * pairs):
        qt[h // 2, :, (h % 2) * B : (h % 2 + 1) * B] = qv[:, h * HEAD : (h + 1) * HEAD].T
    m_ref[...] = jnp.full(m_ref.shape, NEG, F32)
    l_ref[...] = jnp.zeros(l_ref.shape, F32)

    def attend(slot):
        jpos = lax.rem(seq - slot + S, S) * B + jrow
        allowed = (jpos >= start) & (jpos <= ipos)
        bias = jnp.where(allowed, 0.0, NEG).astype(F32)
        bias_ref[...] = jnp.concatenate([bias, bias], axis=1)

        def pair(hp, carry):
            g = lax.div(hp, per_kv)
            x = dot(kbuf[slot, g], qt[hp]) * scale + bias_ref[...]
            old = m_ref[hp]
            new = jnp.maximum(old, jnp.max(x, axis=0, keepdims=True))
            w = jnp.exp2(x - new)
            l_ref[hp] = l_ref[hp] * jnp.exp2(old - new) + jnp.sum(w, axis=0, keepdims=True)
            w_ref[slot, hp] = w.astype(BF16)
            m_ref[hp] = new
            ms_ref[slot, hp] = new
            return carry

        lax.fori_loop(0, pairs, pair, 0)

    def attend_on_arrival(slot):
        @pl.when(seq >= slot)
        def _():
            k_arrive(slot)
            attend(slot)

    attend(0)
    greeted = 2 * near + T + D - 2
    if remotes:
        greeted = greeted + ((seq >= remotes[0]) & (seq <= remotes[-1])).astype(jnp.int32)
    pl.semaphore_wait(barrier, greeted)
    pass_down(0)
    for c in tree.wrapped:
        @pl.when(seq == c)
        def _(c=c):
            far_copy(c, c, last).start()

    ready("n")
    xa_buf[0] = dot_general(down[...], nv[...], NT).astype(BF16)

    def xa_copy(k):
        return remote(
            xa_buf.at[0], xa_buf.at[k], xa_send.at[k], xa_recv.at[k], {"tensor": lax.rem(ten + k, T)}
        )

    send([xa_copy(k) for k in range(1, T)], "xa")

    ready("w")

    def dequantised(first, n, put):
        def one(i, carry):
            row = pl.multiple_of(first + i * GROUP, GROUP)
            block = codes[pl.ds(row, GROUP), :].astype(F32)
            put(i, (block * scales[pl.ds(lax.div(row, GROUP), 1), :]).astype(BF16))
            return carry
        lax.fori_loop(0, n // GROUP, one, 0)

    def w_copy(k):
        return remote(
            wst.at[k], wfull.at[k, core], w_send.at[k], w_recv.at[k], {"tensor": lax.rem(ten + k, T)}
        )

    def wc_copy(k, h):
        return remote(wfull.at[k, h], wfull.at[k, h], wc_send.at[k], wc_recv.at[k], {"dp": sibling})

    for k in range(1, T):
        def put(i, value, k=k):
            wst[k, pl.ds(pl.multiple_of(i * GROUP, GROUP), GROUP), :] = value
        dequantised(lax.rem(ten + k, T) * feats + core * hf, hf, put)
        send([w_copy(k)])
    coming["w"] = [w_copy(k) for k in range(1, T)]
    for h in range(2):
        def put(i, value, h=h):
            wfull[0, h, pl.ds(pl.multiple_of(i * GROUP, GROUP), GROUP), :] = value
        dequantised(ten * feats + h * hf, hf, put)

    for a in tree.relays:
        @pl.when(runs(a))
        def _(a=a):
            k_arrive(a)
            pass_down(a)
            @pl.when(seq >= a)
            def _():
                attend(a)
        for b in tree.after[a]:
            attend_on_arrival(b)
        for plane in tree.far_relays[a]:
            @pl.when(seq == plane)
            def _(plane=plane):
                pass_far(plane)
    relay = seq < 0
    for plane in tree.far_planes:
        relay = relay | (seq == plane)

    def far_slot(i, carry):
        slot = last - i

        @pl.when(seq >= slot)
        def _():
            @pl.when(jnp.logical_not(relay & (seq - slot <= tree.wrapped[-1])))
            def _():
                k_arrive(slot)
            attend(slot)
        return carry

    lax.fori_loop(0, last - half, far_slot, 0)
    for b in tree.final:
        attend_on_arrival(b)

    l_ref[...] = 1.0 / l_ref[...]
    ready("g")

    def partial(slot):
        for g in range(KV):
            total = None
            for i in range(per_kv):
                hp = g * per_kv + i
                factor = jnp.exp2(ms_ref[slot, hp] - m_ref[hp]) * l_ref[hp]
                p = (w_ref[slot, hp].astype(F32) * factor).astype(BF16)
                one = dot(p, gv[hp])
                total = one if total is None else total + one
            acc_ref[g] = total

    def s_copy(a, b, where):
        return remote(rs_out.at[b], rs_in.at[b], s_send.at[b], s_recv.at[b], {"seq": where})

    def up_to(a, b):
        return s_copy(a, b, lax.rem(seq + a - b + S, S))

    def gather(a, keep):
        if a == 0:
            partial(0)
        else:
            @pl.when(seq >= a)
            def _():
                partial(a)

            @pl.when(seq < a)
            def _():
                acc_ref[...] = jnp.zeros(acc_ref.shape, F32)
        for b in tree.children[a]:
            @pl.when(lax.rem(seq - a + S, S) + tree.least[b] <= last)
            def _(b=b):
                s_copy(a, b, seq).wait_recv()
                acc_ref[...] += rs_in[b].astype(F32)
        if keep:
            rs_out[a] = acc_ref[...].astype(BF16)

    def far_up(c, a, b):
        slot, e = b - c, tree.far_index[a, b, c]
        return remote(
            rs_out.at[slot], rs_far.at[e], s_send.at[slot], far_recv.at[e], {"seq": jnp.int32(a)}
        )

    def send_up(b):
        @pl.when(runs(b))
        def _():
            gather(b, True)
            up_to(tree.parent[b], b).start()

    def far_leaf(c, a, b):
        partial(b - c)
        rs_out[b - c] = acc_ref[...].astype(BF16)
        far_up(c, a, b).start()

    def far_gather(a, c):
        partial(a - c)
        for b in tree.far_children(a, c):
            far_up(c, a, b).wait_recv()
            acc_ref[...] += rs_far[tree.far_index[a, b, c]].astype(F32)
        rs_out[a - c] = acc_ref[...].astype(BF16)
        far_up(c, tree.far_parent(a, c), a).start()

    for b in reversed(tree.final):
        send_up(b)
    for plane in tree.far_leaves:
        @pl.when(seq == plane)
        def _(plane=plane):
            for c in reversed(tree.wrapped):
                a = tree.far_parent(plane, c)
                if a is not None:
                    far_leaf(c, a, plane)
    for a in reversed(tree.relays):
        for plane in tree.far_relays[a]:
            @pl.when(seq == plane)
            def _(plane=plane):
                for c in reversed(tree.wrapped):
                    if tree.far_parent(plane, c) is not None:
                        far_gather(plane, c)
        for b in tree.after[a]:
            send_up(b)
        send_up(a)

    arrive("xa")
    xat = xa_buf[0].astype(F32)
    for k in range(1, T):
        xat = xat + xa_buf[k].astype(F32)
    xat = xat.astype(BF16)
    arrive("w")
    send([wc_copy(k, core) for k in range(1, T)])
    coming["wc"] = [wc_copy(k, 1 - core) for k in range(1, T)]
    ready("up")
    gather(0, False)
    for c in tree.wrapped:
        @pl.when(seq == c)
        def _(c=c):
            far_up(c, c, last).wait_recv()
            acc_ref[...] += rs_far[tree.far_index[c, last, c]].astype(F32)
    for g in range(KV):
        dv_buf[0, :, g * HEAD : (g + 1) * HEAD] = acc_ref[g].astype(BF16)

    dv = dv_buf[0]
    gx_buf[0] = dot_general(up[...], dv, NT).astype(BF16)

    def gx_copy(k):
        return remote(
            gx_buf.at[0], gx_buf.at[k], gx_send.at[k], gx_recv.at[k], {"tensor": lax.rem(ten + k, T)}
        )

    def dv_copy(k):
        return remote(
            dv_buf.at[0], dv_buf.at[k], dv_send.at[k], dv_recv.at[k], {"tensor": lax.rem(ten + k, T)}
        )

    send([gx_copy(k) for k in range(1, T)], "gx")
    send([dv_copy(k) for k in range(1, T)], "dv")
    per = a_src.shape[1]
    across = (feats + cols) // 128

    def tile_at(i, j):
        n = i * across + j
        return n // per, n % per

    part_b = dot(xat, dv)
    for i in range(rank // 16):
        for j in range(cols // 128):
            p, q = tile_at(i, feats // 128 + j)
            a_src[p, q] = part_b[i * 16 : i * 16 + 16, j * 128 : j * 128 + 128].astype(BF16)
    arrive("gx")
    gpt = gx_buf[0].astype(F32)
    for k in range(1, T):
        gpt = gpt + gx_buf[k].astype(F32)
    gpt = gpt.astype(BF16)
    for j in range(feats // 128):
        part_a = dot(gpt, nv[:, j * 128 : j * 128 + 128])
        for i in range(rank // 16):
            p, q = tile_at(i, j)
            a_src[p, q] = part_a[i * 16 : i * 16 + 16].astype(BF16)

    def a_copy(k):
        peer = lax.rem(dp + k, D)
        return remote(a_src.at[peer], a_rcv.at[k], a_send.at[k], a_recv.at[k], {"dp": peer})

    send([a_copy(k) for k in range(1, D)], "a")
    arrive("a")
    total = a_src[dp].astype(F32)
    for k in range(1, D):
        total = total + a_rcv[k].astype(F32)
    b_src[...] = total.astype(BF16)

    owners = [j * S // per for j in range(per)]

    def b_copy(j):
        away = lax.rem(owners[j] - seq + S, S)
        return remote(
            b_src.at[j], b_rcv.at[away], b_send.at[j], b_recv.at[away], {"seq": jnp.int32(owners[j])}
        )

    mine = jnp.int32(0)
    owner = seq == owners[0]
    for j in range(1, per):
        mine = jnp.where(seq == owners[j], j, mine)
        owner = owner | (seq == owners[j])

    for j in range(per):
        @pl.when(seq != owners[j])
        def _():
            b_copy(j).start()

    def c_copy(k):
        return remote(
            c_buf.at[mine], c_buf.at[mine], c_send.at[k], c_recv.at[mine], {"seq": lax.rem(seq + k, S)}
        )

    @pl.when(owner)
    def _():
        total = b_src[mine].astype(F32)
        for k in range(1, S):
            remote(
                b_src.at[0], b_rcv.at[k], b_send.at[0], b_recv.at[k], {"seq": lax.rem(seq + k, S)}
            ).wait_recv()
            total = total + b_rcv[k].astype(F32)
        c_buf[mine] = total.astype(BF16)
        for k in range(1, S):
            c_copy(k).start()

    for j in range(per):
        @pl.when(seq != owners[j])
        def _():
            remote(
                b_src.at[j], c_buf.at[j], c_send.at[0], c_recv.at[j], {"seq": jnp.int32(owners[j])}
            ).wait_recv()

    def d_copy(k):
        return remote(
            c_buf, d_buf.at[dp], d_send.at[k], d_recv.at[dp], {"dp": lax.rem(dp + k, D)}
        )

    send([d_copy(k) for k in range(1, D)])

    def d_from(k):
        peer = lax.rem(dp + k, D)
        return remote(c_buf, d_buf.at[peer], d_send.at[k], d_recv.at[peer], {"dp": peer})

    coming["d"] = [d_from(k) for k in range(1, D)]
    d_buf[dp] = c_buf[...]

    gp = gpt.T
    arrive("dv")
    arrive("wc")
    width = min(256, hf)
    for n in range(feats // width):
        h, row = n * width // hf, n * width % hf
        at = slice(n * width, (n + 1) * width)
        total = 2.0 * dot(gp, down[:, at])
        for k in range(T):
            total = total + dot_general(dv_buf[k], wfull[k, h, row : row + width, :], NT)
        dn_ref[:, at] = total.astype(BF16)

    arrive("d")
    factor = 2.0 / math.sqrt(D * S * B)
    for i in range(rank // 16):
        for j in range(across):
            p, q = tile_at(i, j)
            value = d_buf[p, q].astype(F32) * factor
            if j < feats // 128:
                ga_ref[i * 16 : i * 16 + 16, j * 128 : j * 128 + 128] = value
            else:
                c = j * 128 - feats
                gb_ref[i * 16 : i * 16 + 16, c : c + 128] = value

    for c in sent:
        c.wait_send()
    for b in range(1, half + 1):
        a = tree.parent[b]

        @pl.when(lax.rem(seq - a + S, S) + tree.least[b] <= last)
        def _(a=a, b=b):
            k_copy(a, b, seq).wait_send()

        @pl.when(runs(b))
        def _(b=b):
            up_to(a, b).wait_send()
    for c in tree.wrapped:
        for a, b in tree.far_edges(c):
            @pl.when(seq == a)
            def _(a=a, b=b, c=c):
                far_copy(c, a, b).wait_send()

            @pl.when(seq == b)
            def _(a=a, b=b, c=c):
                far_up(c, a, b).wait_send()
    for j in range(per):
        @pl.when(seq != owners[j])
        def _():
            b_copy(j).wait_send()

    @pl.when(owner)
    def _():
        for k in range(1, S):
            c_copy(k).wait_send()


def body(
    shape, queries, keys, output_gradient, normed, document_length, codes, scales,
    adapter_down, adapter_up,
):
    D, S, T = shape
    B = queries.shape[1]
    heads = queries.shape[2] // HEAD
    pairs = heads // 2
    feats = normed.shape[2]
    rank, cols = adapter_up.shape
    half = S // 2
    far = Tree(S).far_most
    per = (rank // 16) * ((feats + cols) // 128) // D
    hbm = pl.BlockSpec(memory_space=pltpu.HBM)
    vmem = pl.BlockSpec(memory_space=pltpu.VMEM)
    dma = pltpu.SemaphoreType.DMA
    d_normed, grad_a, grad_b = pl.pallas_call(
        functools.partial(kernel, shape),
        out_shape=(
            jax.ShapeDtypeStruct((B, feats), BF16),
            jax.ShapeDtypeStruct((rank, feats), F32),
            jax.ShapeDtypeStruct((rank, cols), F32),
        ),
        in_specs=[hbm] * 9,
        out_specs=(vmem, vmem, vmem),
        scratch_shapes=[
            pltpu.SMEM(document_length.shape, jnp.int32),
            pltpu.VMEM((S, KV, B, HEAD), BF16),
            pltpu.VMEM((B, heads * HEAD), BF16),
            pltpu.VMEM((pairs, HEAD, 2 * B), BF16),
            pltpu.VMEM((pairs, 2 * B, HEAD), BF16),
            pltpu.VMEM((B, feats), BF16),
            pltpu.VMEM(codes.shape, BF16),
            pltpu.VMEM(scales.shape, F32),
            pltpu.VMEM((rank, feats), BF16),
            pltpu.VMEM((rank, cols), BF16),
            pltpu.VMEM((T, feats // 2, cols), BF16),
            pltpu.VMEM((T, 2, feats // 2, cols), BF16),
            pltpu.VMEM((B, 2 * B), F32),
            pltpu.VMEM((pairs, 1, 2 * B), F32),
            pltpu.VMEM((pairs, 1, 2 * B), F32),
            pltpu.VMEM((S, pairs, 1, 2 * B), F32),
            pltpu.VMEM((S, pairs, B, 2 * B), BF16),
            pltpu.VMEM((KV, B, HEAD), F32),
            pltpu.VMEM((S, KV, B, HEAD), BF16),
            pltpu.VMEM((half + 1, KV, B, HEAD), BF16),
            pltpu.VMEM((far, KV, B, HEAD), BF16),
            pltpu.VMEM((T, rank, B), BF16),
            pltpu.VMEM((T, rank, B), BF16),
            pltpu.VMEM((T, B, cols), BF16),
            pltpu.VMEM((D, per, 16, 128), BF16),
            pltpu.VMEM((D, per, 16, 128), BF16),
            pltpu.VMEM((per, 16, 128), BF16),
            pltpu.VMEM((S, 16, 128), BF16),
            pltpu.VMEM((per, 16, 128), BF16),
            pltpu.VMEM((D, per, 16, 128), BF16),
            dma((9 + heads,)),
            dma((S + far,)),
            dma((S,)),
            dma((S,)),
            dma((half + 1,)),
            dma((far,)),
            dma((T,)),
            dma((T,)),
            dma((T,)),
            dma((T,)),
            dma((T,)),
            dma((T,)),
            dma((T,)),
            dma((T,)),
            dma((T,)),
            dma((T,)),
            dma((D,)),
            dma((D,)),
            dma((per,)),
            dma((S,)),
            dma((S,)),
            dma((per,)),
            dma((D,)),
            dma((D,)),
        ],
        compiler_params=pltpu.CompilerParams(
            collective_id=0, has_side_effects=True, vmem_limit_bytes=40 * 1024 * 1024
        ),
        name="value_backward",
    )(
        *(
            pltpu.with_memory_space_constraint(x, pltpu.HBM)
            for x in (
                queries[0], keys[0], output_gradient[0], normed[0], document_length, codes,
                scales, adapter_down.T, adapter_up,
            )
        )
    )
    return d_normed[None], grad_a.T, grad_b


def solution(mesh):
    shape = tuple(mesh.shape[a] for a in ("dp", "seq", "tensor"))
    split = P("dp", "seq", "tensor")
    placed = (
        split, split, split, split,
        P("dp", None), P(None, "tensor"), P(None, "tensor"), P("tensor", None), P(None, "tensor"),
    )
    return jax.shard_map(
        functools.partial(body, shape),
        mesh=mesh,
        in_specs=placed,
        out_specs=(split, P("tensor", None), P(None, "tensor")),
        check_vma=False,
    )
```

time: 114 us -> 109 us (0.956)
  local copies, waits for them, and re-layouts: 10.6 us -> 2.04 us
  Pallas kernels: 102 us -> 106 us
    unnamed x21 -> x3, local copies, waits for them, and re-layouts: 10.6 us -> 2.04 us
    pallas_call x1, Pallas kernels: 102 us -> 106 us  [body(): pl.pallas_call(functools.partial(kernel, shape), out_shape=(jax.ShapeDtyp...]
where the time goes in v2:
time: 109 us
  Pallas kernels  106 us (97%)
  local copies, waits for them, and re-layouts  2.04 us (2%)
    pallas_call x1, Pallas kernels, body(): pl.pallas_call(functools.partial(kernel, shape), out_shape=(jax.ShapeDtyp...  106 us

profile of v2, /device:TPU:1, one launch (start us, length us, event | category | flops | bytes accessed | tf_op | source)
XLA Modules:
  0.0 109.0 jit_solution(13720550224513192748)
XLA Ops:
  0.6 106.3 %value_backward.1 = (bf16[128,1024]{1,0:T(8,128)(2,1)S(1)}, f32[64,1024]{1,0:T(8,128)S(1)}, f32[64,256]{1,0:T(8,128)S(1)}) custom-call(bf16[128,2048]{1,0:T(8,128)(2,1)} %bitcast.9, bf16[128,256]{1,0:T(8,128)(2,1)} %bitcast.13, bf16[128,2048]{1,0:T(8,128)(2,1)} %bitcast.10, bf16[128,1024]{1,0:T(8,128)(2,1)} %bitcast.11, s32[1,8]{1,0:T(1,128)} %len_hbm.1, ...), custom_call_target="tpu_custom_call" | custom-call | tf_op jit(solution)/shard_map/value_backward/pallas_call | solution.py:618
  106.9 0.7 copy.15
  107.6 0.7 copy.16
  108.3 0.6 copy.17

commit v3 on v2

--- a/solution.py
+++ b/solution.py
@@ -29,51 +29,26 @@
 
 class Tree:
     def __init__(self, size):
-        half, last = size // 2, size - 1
         if size == 16:
-            self.parent = {3: 0, 1: 0, 6: 3, 2: 3, 8: 6, 4: 6, 7: 6, 5: 6}
-            self.after = {3: [1], 6: [2]}
-            self.far_relays = {3: [15], 6: [12]}
-            self.final = [7, 5, 8, 4]
-            self.far_planes = [15, 12]
-            self.far_leaves = [14, 13, 11, 10, 9]
+            self.parent = {3: 0, 1: 0, 11: 0, 6: 3, 2: 3, 12: 11, 10: 11, 9: 11, 8: 6, 4: 6, 7: 6, 5: 6}
+            self.after = {3: [], 11: [3, 1, 11], 6: [2, 6]}
+            self.final = [12, 10, 9, 7, 5, 8, 4]
+            self.near = [1, 2, 3]
+            self.up = [8, 4, 7, 5, 12, 10, 9, 2, 1, 6, 11, 3]
+            self.far = 11
         else:
-            self.parent = {2: 0, 1: 2}
-            self.after = {2: []}
-            self.far_relays = {2: [last]}
-            self.final = [1]
-            self.far_planes = [last]
-            self.far_leaves = []
+            self.parent = {2: 0, 1: 2, 3: 0}
+            self.after = {2: [2]}
+            self.final = [1, 3]
+            self.near = [1, 2]
+            self.up = [1, 3, 2]
+            self.far = None
         self.relays = list(self.after)
-        self.children = {a: [b for b in self.parent if self.parent[b] == a] for a in range(half + 1)}
+        self.children = {a: [b for b in self.parent if self.parent[b] == a] for a in range(size)}
         self.least = {b: min(self.below(b)) for b in self.parent}
-        self.wrapped = list(range(half - 1))
-        self.last = last
-        self.half = half
-        self.far_index = {}
-        for a in range(size):
-            edges = [(b, c) for c in self.wrapped for (x, b) in self.far_edges(c) if x == a]
-            for e, (b, c) in enumerate(edges):
-                self.far_index[a, b, c] = e
-        self.far_most = max(self.far_index.values()) + 1
 
     def below(self, b):
         return [b] + [x for child in self.children[b] for x in self.below(child)]
-
-    def far_parent(self, plane, c):
-        if plane - c <= self.half:
-            return None
-        if plane == self.last:
-            return c
-        if plane in (14, 12) or (plane, c) == (13, 4):
-            return 15
-        return 12
-
-    def far_edges(self, c):
-        return [(self.far_parent(b, c), b) for b in range(c + self.half + 1, self.last + 1)]
-
-    def far_children(self, plane, c):
-        return [b for a, b in self.far_edges(c) if a == plane]
 
 
 def kernel(
@@ -81,14 +56,13 @@
     q_hbm, k_hbm, g_hbm, n_hbm, len_hbm, codes_hbm, scales_hbm, down_hbm, up_hbm,
     dn_ref, ga_ref, gb_ref,
     len_ref, kbuf, qv, qt, gv, nv, codes, scales, down, up, wst, wfull, bias_ref,
-    m_ref, l_ref, ms_ref, w_ref, acc_ref, rs_out, rs_in, rs_far, xa_buf, gx_buf, dv_buf,
+    m_ref, l_ref, ms_ref, w_ref, acc_ref, rs_out, rs_in, xa_buf, gx_buf, dv_buf,
     a_src, a_rcv, b_src, b_rcv, c_buf, d_buf,
-    local_sem, k_send, k_recv, s_send, s_recv, far_recv,
+    local_sem, k_send, k_recv, s_send, s_recv,
     w_send, w_recv, wc_send, wc_recv, xa_send, xa_recv, gx_send, gx_recv,
     dv_send, dv_recv, a_send, a_recv, b_send, b_recv, c_send, c_recv, d_send, d_recv,
 ):
     D, S, T = shape
-    half = S // 2
     tree = Tree(S)
     B = kbuf.shape[2]
     pairs = qt.shape[0]
@@ -102,7 +76,6 @@
     ten = lax.axis_index("tensor")
     core = lax.rem(dp, 2)
     sibling = dp + 1 - 2 * core
-    near = min(3, half)
     last = S - 1
 
     def remote(src, dst, send, recv, where):
@@ -164,21 +137,22 @@
             return carry
         lax.fori_loop(1, size, one, 0)
 
-    for k in range(1, near + 1):
+    for k in tree.near:
         for away in (k, S - k):
             pl.semaphore_signal(
                 barrier, inc=1, device_id={"seq": lax.rem(seq + away, S)}, device_id_type=MESH
             )
     greet("tensor", ten, T)
     greet("dp", dp, D)
-    remotes = [c for c in tree.wrapped if near <= c < last - near]
-    if remotes:
-        @pl.when(seq == last)
+    greeted = 2 * len(tree.near) + T + D - 2
+    if tree.far:
+        owner_there = lax.rem(seq - tree.far + S, S)
+
+        @pl.when(owner_there + tree.least[tree.far] <= last)
         def _():
-            for c in remotes:
-                pl.semaphore_signal(
-                    barrier, inc=1, device_id={"seq": jnp.int32(c)}, device_id_type=MESH
-                )
+            pl.semaphore_signal(barrier, inc=1, device_id={"seq": owner_there}, device_id_type=MESH)
+
+        greeted = greeted + (seq + tree.least[tree.far] <= last).astype(jnp.int32)
 
     def k_copy(a, b, where):
         return remote(kbuf.at[a], kbuf.at[b], k_send.at[b], k_recv.at[b], {"seq": where})
@@ -194,21 +168,6 @@
 
     def k_arrive(b):
         k_copy(0, b, seq).wait_recv()
-
-    def far_copy(c, a, b):
-        here, there = a - c, b - c
-        return remote(
-            kbuf.at[here], kbuf.at[there], k_send.at[S + tree.far_index[a, b, c]], k_recv.at[there],
-            {"seq": jnp.int32(b)},
-        )
-
-    def pass_far(a):
-        for c in tree.wrapped:
-            if tree.far_parent(a, c) is None:
-                continue
-            k_arrive(a - c)
-            for b in tree.far_children(a, c):
-                far_copy(c, a, b).start()
 
     ready("q")
     ready("k")
@@ -232,9 +191,8 @@
         bias = jnp.where(allowed, 0.0, NEG).astype(F32)
         bias_ref[...] = jnp.concatenate([bias, bias], axis=1)
 
-        def pair(hp, carry):
-            g = lax.div(hp, per_kv)
-            x = dot(kbuf[slot, g], qt[hp]) * scale + bias_ref[...]
+        for hp in range(pairs):
+            x = dot(kbuf[slot, hp // per_kv], qt[hp]) * scale + bias_ref[...]
             old = m_ref[hp]
             new = jnp.maximum(old, jnp.max(x, axis=0, keepdims=True))
             w = jnp.exp2(x - new)
@@ -242,9 +200,6 @@
             w_ref[slot, hp] = w.astype(BF16)
             m_ref[hp] = new
             ms_ref[slot, hp] = new
-            return carry
-
-        lax.fori_loop(0, pairs, pair, 0)
 
     def attend_on_arrival(slot):
         @pl.when(seq >= slot)
@@ -253,15 +208,8 @@
             attend(slot)
 
     attend(0)
-    greeted = 2 * near + T + D - 2
-    if remotes:
-        greeted = greeted + ((seq >= remotes[0]) & (seq <= remotes[-1])).astype(jnp.int32)
     pl.semaphore_wait(barrier, greeted)
     pass_down(0)
-    for c in tree.wrapped:
-        @pl.when(seq == c)
-        def _(c=c):
-            far_copy(c, c, last).start()
 
     ready("n")
     xa_buf[0] = dot_general(down[...], nv[...], NT).astype(BF16)
@@ -291,47 +239,36 @@
     def wc_copy(k, h):
         return remote(wfull.at[k, h], wfull.at[k, h], wc_send.at[k], wc_recv.at[k], {"dp": sibling})
 
-    for k in range(1, T):
-        def put(i, value, k=k):
+    def send_weights(k):
+        def put(i, value):
             wst[k, pl.ds(pl.multiple_of(i * GROUP, GROUP), GROUP), :] = value
         dequantised(lax.rem(ten + k, T) * feats + core * hf, hf, put)
         send([w_copy(k)])
-    coming["w"] = [w_copy(k) for k in range(1, T)]
-    for h in range(2):
-        def put(i, value, h=h):
-            wfull[0, h, pl.ds(pl.multiple_of(i * GROUP, GROUP), GROUP), :] = value
-        dequantised(ten * feats + h * hf, hf, put)
-
-    for a in tree.relays:
+
+    def own_weights():
+        for h in range(2):
+            def put(i, value, h=h):
+                wfull[0, h, pl.ds(pl.multiple_of(i * GROUP, GROUP), GROUP), :] = value
+            dequantised(ten * feats + h * hf, hf, put)
+
+
+    for n, a in enumerate(tree.relays):
         @pl.when(runs(a))
         def _(a=a):
             k_arrive(a)
             pass_down(a)
-            @pl.when(seq >= a)
-            def _():
-                attend(a)
+        if n + 1 < T:
+            send_weights(n + 1)
         for b in tree.after[a]:
-            attend_on_arrival(b)
-        for plane in tree.far_relays[a]:
-            @pl.when(seq == plane)
-            def _(plane=plane):
-                pass_far(plane)
-    relay = seq < 0
-    for plane in tree.far_planes:
-        relay = relay | (seq == plane)
-
-    def far_slot(i, carry):
-        slot = last - i
-
-        @pl.when(seq >= slot)
-        def _():
-            @pl.when(jnp.logical_not(relay & (seq - slot <= tree.wrapped[-1])))
-            def _():
-                k_arrive(slot)
-            attend(slot)
-        return carry
-
-    lax.fori_loop(0, last - half, far_slot, 0)
+            if b in tree.relays:
+                @pl.when(seq >= b)
+                def _(b=b):
+                    attend(b)
+            else:
+                attend_on_arrival(b)
+    for k in range(len(tree.relays) + 1, T):
+        send_weights(k)
+    coming["w"] = [w_copy(k) for k in range(1, T)]
     for b in tree.final:
         attend_on_arrival(b)
 
@@ -374,50 +311,11 @@
         if keep:
             rs_out[a] = acc_ref[...].astype(BF16)
 
-    def far_up(c, a, b):
-        slot, e = b - c, tree.far_index[a, b, c]
-        return remote(
-            rs_out.at[slot], rs_far.at[e], s_send.at[slot], far_recv.at[e], {"seq": jnp.int32(a)}
-        )
-
-    def send_up(b):
+    for b in tree.up:
         @pl.when(runs(b))
-        def _():
+        def _(b=b):
             gather(b, True)
             up_to(tree.parent[b], b).start()
-
-    def far_leaf(c, a, b):
-        partial(b - c)
-        rs_out[b - c] = acc_ref[...].astype(BF16)
-        far_up(c, a, b).start()
-
-    def far_gather(a, c):
-        partial(a - c)
-        for b in tree.far_children(a, c):
-            far_up(c, a, b).wait_recv()
-            acc_ref[...] += rs_far[tree.far_index[a, b, c]].astype(F32)
-        rs_out[a - c] = acc_ref[...].astype(BF16)
-        far_up(c, tree.far_parent(a, c), a).start()
-
-    for b in reversed(tree.final):
-        send_up(b)
-    for plane in tree.far_leaves:
-        @pl.when(seq == plane)
-        def _(plane=plane):
-            for c in reversed(tree.wrapped):
-                a = tree.far_parent(plane, c)
-                if a is not None:
-                    far_leaf(c, a, plane)
-    for a in reversed(tree.relays):
-        for plane in tree.far_relays[a]:
-            @pl.when(seq == plane)
-            def _(plane=plane):
-                for c in reversed(tree.wrapped):
-                    if tree.far_parent(plane, c) is not None:
-                        far_gather(plane, c)
-        for b in tree.after[a]:
-            send_up(b)
-        send_up(a)
 
     arrive("xa")
     xat = xa_buf[0].astype(F32)
@@ -429,11 +327,6 @@
     coming["wc"] = [wc_copy(k, 1 - core) for k in range(1, T)]
     ready("up")
     gather(0, False)
-    for c in tree.wrapped:
-        @pl.when(seq == c)
-        def _(c=c):
-            far_up(c, c, last).wait_recv()
-            acc_ref[...] += rs_far[tree.far_index[c, last, c]].astype(F32)
     for g in range(KV):
         dv_buf[0, :, g * HEAD : (g + 1) * HEAD] = acc_ref[g].astype(BF16)
 
@@ -480,6 +373,7 @@
         return remote(a_src.at[peer], a_rcv.at[k], a_send.at[k], a_recv.at[k], {"dp": peer})
 
     send([a_copy(k) for k in range(1, D)], "a")
+    own_weights()
     arrive("a")
     total = a_src[dp].astype(F32)
     for k in range(1, D):
@@ -569,8 +463,7 @@
 
     for c in sent:
         c.wait_send()
-    for b in range(1, half + 1):
-        a = tree.parent[b]
+    for b, a in tree.parent.items():
 
         @pl.when(lax.rem(seq - a + S, S) + tree.least[b] <= last)
         def _(a=a, b=b):
@@ -579,15 +472,6 @@
         @pl.when(runs(b))
         def _(b=b):
             up_to(a, b).wait_send()
-    for c in tree.wrapped:
-        for a, b in tree.far_edges(c):
-            @pl.when(seq == a)
-            def _(a=a, b=b, c=c):
-                far_copy(c, a, b).wait_send()
-
-            @pl.when(seq == b)
-            def _(a=a, b=b, c=c):
-                far_up(c, a, b).wait_send()
     for j in range(per):
         @pl.when(seq != owners[j])
         def _():
@@ -609,8 +493,6 @@
     pairs = heads // 2
     feats = normed.shape[2]
     rank, cols = adapter_up.shape
-    half = S // 2
-    far = Tree(S).far_most
     per = (rank // 16) * ((feats + cols) // 128) // D
     hbm = pl.BlockSpec(memory_space=pltpu.HBM)
     vmem = pl.BlockSpec(memory_space=pltpu.VMEM)
@@ -644,8 +526,7 @@
             pltpu.VMEM((S, pairs, B, 2 * B), BF16),
             pltpu.VMEM((KV, B, HEAD), F32),
             pltpu.VMEM((S, KV, B, HEAD), BF16),
-            pltpu.VMEM((half + 1, KV, B, HEAD), BF16),
-            pltpu.VMEM((far, KV, B, HEAD), BF16),
+            pltpu.VMEM((S, KV, B, HEAD), BF16),
             pltpu.VMEM((T, rank, B), BF16),
             pltpu.VMEM((T, rank, B), BF16),
             pltpu.VMEM((T, B, cols), BF16),
@@ -656,11 +537,10 @@
             pltpu.VMEM((per, 16, 128), BF16),
             pltpu.VMEM((D, per, 16, 128), BF16),
             dma((9 + heads,)),
-            dma((S + far,)),
             dma((S,)),
             dma((S,)),
-            dma((half + 1,)),
-            dma((far,)),
+            dma((S,)),
+            dma((S,)),
             dma((T,)),
             dma((T,)),
             dma((T,)),

time: 109 us -> 88.5 us (0.81)
  Pallas kernels: 106 us -> 85.7 us
    pallas_call x1, Pallas kernels: 106 us -> 85.7 us  [body(): pl.pallas_call(functools.partial(kernel, shape), out_shape=(jax.ShapeDtyp...]
where the time goes in v3:
time: 88.5 us; the launch traced here: 88.4 us
  Pallas kernels  85.7 us (97%)
  local copies, waits for them, and re-layouts  2.04 us (2%)
    pallas_call x1, Pallas kernels, body(): pl.pallas_call(functools.partial(kernel, shape), out_shape=(jax.ShapeDtyp...  85.7 us
    unnamed x3, local copies, waits for them, and re-layouts  2.04 us

profile of v3, /device:TPU:1, one launch (start us, length us, event | category | flops | bytes accessed | tf_op | source)
XLA Modules:
  0.0 88.4 jit_solution(12536538764662562376)
XLA Ops:
  0.6 85.7 %value_backward.1 = (bf16[128,1024]{1,0:T(8,128)(2,1)S(1)}, f32[64,1024]{1,0:T(8,128)S(1)}, f32[64,256]{1,0:T(8,128)S(1)}) custom-call(bf16[128,2048]{1,0:T(8,128)(2,1)} %bitcast.9, bf16[128,256]{1,0:T(8,128)(2,1)} %bitcast.13, bf16[128,2048]{1,0:T(8,128)(2,1)} %bitcast.10, bf16[128,1024]{1,0:T(8,128)(2,1)} %bitcast.11, s32[1,8]{1,0:T(1,128)} %len_hbm.1, ...), custom_call_target="tpu_custom_call" | custom-call | tf_op jit(solution)/shard_map/value_backward/pallas_call | solution.py:500
  86.3 0.7 copy.15
  87.0 0.7 copy.16
  87.7 0.6 copy.17

commit v4 on v3

--- a/solution.py
+++ b/solution.py
@@ -12,6 +12,7 @@
 HEAD = 128
 GROUP = 128
 KV = 2
+QUAD = 4
 NEG = -1e30
 F32 = jnp.float32
 BF16 = jnp.bfloat16
@@ -30,22 +31,22 @@
 class Tree:
     def __init__(self, size):
         if size == 16:
-            self.parent = {3: 0, 1: 0, 11: 0, 6: 3, 2: 3, 12: 11, 10: 11, 9: 11, 8: 6, 4: 6, 7: 6, 5: 6}
-            self.after = {3: [], 11: [3, 1, 11], 6: [2, 6]}
+            self.parent = {3: 0, 1: 0, 13: 0, 6: 3, 2: 3, 11: 13, 12: 13, 10: 11, 9: 11}
+            self.parent.update({8: 6, 4: 6, 7: 6, 5: 6})
+            self.after = {3: [], 13: [3, 1], 11: [11, 2], 6: [6]}
             self.final = [12, 10, 9, 7, 5, 8, 4]
-            self.near = [1, 2, 3]
-            self.up = [8, 4, 7, 5, 12, 10, 9, 2, 1, 6, 11, 3]
-            self.far = 11
+            self.up = [8, 4, 7, 5, 10, 9, 12, 2, 1, 6, 11, 3, 13]
+            self.passing = [13]
         else:
-            self.parent = {2: 0, 1: 2, 3: 0}
-            self.after = {2: [2]}
-            self.final = [1, 3]
-            self.near = [1, 2]
-            self.up = [1, 3, 2]
-            self.far = None
+            self.parent = {b: b - 1 for b in range(1, size)}
+            self.after = {b: [b] for b in range(1, size - 1)}
+            self.final = [size - 1]
+            self.up = list(range(size - 1, 0, -1))
+            self.passing = []
+        self.near = [k for k in (1, 2, 3) if 2 * k <= size]
         self.relays = list(self.after)
         self.children = {a: [b for b in self.parent if self.parent[b] == a] for a in range(size)}
-        self.least = {b: min(self.below(b)) for b in self.parent}
+        self.least = {b: min(x for x in self.below(b) if x not in self.passing) for b in self.parent}
 
     def below(self, b):
         return [b] + [x for child in self.children[b] for x in self.below(child)]
@@ -57,10 +58,10 @@
     dn_ref, ga_ref, gb_ref,
     len_ref, kbuf, qv, qt, gv, nv, codes, scales, down, up, wst, wfull, bias_ref,
     m_ref, l_ref, ms_ref, w_ref, acc_ref, rs_out, rs_in, xa_buf, gx_buf, dv_buf,
-    a_src, a_rcv, b_src, b_rcv, c_buf, d_buf,
-    local_sem, k_send, k_recv, s_send, s_recv,
+    a_src, a_rcv, b_buf, c_buf, d_buf,
+    met_sem, local_sem, k_send, k_recv, s_send, s_recv,
     w_send, w_recv, wc_send, wc_recv, xa_send, xa_recv, gx_send, gx_recv,
-    dv_send, dv_recv, a_send, a_recv, b_send, b_recv, c_send, c_recv, d_send, d_recv,
+    dv_send, dv_recv, a_send, a_recv, b_send, b_recv, d_send, d_recv,
 ):
     D, S, T = shape
     tree = Tree(S)
@@ -145,15 +146,6 @@
     greet("tensor", ten, T)
     greet("dp", dp, D)
     greeted = 2 * len(tree.near) + T + D - 2
-    if tree.far:
-        owner_there = lax.rem(seq - tree.far + S, S)
-
-        @pl.when(owner_there + tree.least[tree.far] <= last)
-        def _():
-            pl.semaphore_signal(barrier, inc=1, device_id={"seq": owner_there}, device_id_type=MESH)
-
-        greeted = greeted + (seq + tree.least[tree.far] <= last).astype(jnp.int32)
-
     def k_copy(a, b, where):
         return remote(kbuf.at[a], kbuf.at[b], k_send.at[b], k_recv.at[b], {"seq": where})
 
@@ -210,6 +202,10 @@
     attend(0)
     pl.semaphore_wait(barrier, greeted)
     pass_down(0)
+    for k in range(1, D):
+        pl.semaphore_signal(
+            met_sem, inc=1, device_id={"dp": lax.rem(dp + k, D)}, device_id_type=MESH
+        )
 
     ready("n")
     xa_buf[0] = dot_general(down[...], nv[...], NT).astype(BF16)
@@ -295,6 +291,8 @@
     def gather(a, keep):
         if a == 0:
             partial(0)
+        elif a in tree.passing:
+            acc_ref[...] = jnp.zeros(acc_ref.shape, F32)
         else:
             @pl.when(seq >= a)
             def _():
@@ -345,17 +343,29 @@
 
     send([gx_copy(k) for k in range(1, T)], "gx")
     send([dv_copy(k) for k in range(1, T)], "dv")
-    per = a_src.shape[1]
-    across = (feats + cols) // 128
-
-    def tile_at(i, j):
-        n = i * across + j
-        return n // per, n % per
-
+    members = D * QUAD
+    quads = S // QUAD
+    place = lax.rem(seq, QUAD)
+    quad = lax.div(seq, QUAD)
+    mine = dp * QUAD + place
+    wide_a = feats // 128
+    wide_b = cols // 128
+    n_tiles = (rank // 16) * (wide_a + wide_b)
+
+    def tile_a(i, j):
+        n = i * wide_a + j
+        return n % members, n // members
+
+    def tile_b(i, j):
+        n = (rank // 16) * wide_a + i * wide_b + j
+        return n % members, n // members
+
+    for n in range(n_tiles, members * a_src.shape[1]):
+        a_src[n % members, n // members] = jnp.zeros((16, 128), BF16)
     part_b = dot(xat, dv)
     for i in range(rank // 16):
         for j in range(cols // 128):
-            p, q = tile_at(i, feats // 128 + j)
+            p, q = tile_b(i, j)
             a_src[p, q] = part_b[i * 16 : i * 16 + 16, j * 128 : j * 128 + 128].astype(BF16)
     arrive("gx")
     gpt = gx_buf[0].astype(F32)
@@ -365,77 +375,66 @@
     for j in range(feats // 128):
         part_a = dot(gpt, nv[:, j * 128 : j * 128 + 128])
         for i in range(rank // 16):
-            p, q = tile_at(i, j)
+            p, q = tile_a(i, j)
             a_src[p, q] = part_a[i * 16 : i * 16 + 16].astype(BF16)
 
+    def member(k):
+        there = lax.rem(dp + lax.div(k, QUAD), D)
+        at = lax.rem(place + lax.rem(k, QUAD), QUAD)
+        return there * QUAD + at, {"dp": there, "seq": quad * QUAD + at}
+
     def a_copy(k):
-        peer = lax.rem(dp + k, D)
-        return remote(a_src.at[peer], a_rcv.at[k], a_send.at[k], a_recv.at[k], {"dp": peer})
-
-    send([a_copy(k) for k in range(1, D)], "a")
+        piece, where = member(k)
+        return remote(a_src.at[piece], a_rcv.at[k], a_send.at[k], a_recv.at[k], where)
+
+    def each(first, end, act):
+        def one(k, carry):
+            act(k)
+            return carry
+        lax.fori_loop(first, end, one, 0)
+
+    pl.semaphore_wait(met_sem, D - 1)
+    each(1, members, lambda k: a_copy(k).start())
     own_weights()
-    arrive("a")
-    total = a_src[dp].astype(F32)
-    for k in range(1, D):
-        total = total + a_rcv[k].astype(F32)
-    b_src[...] = total.astype(BF16)
-
-    owners = [j * S // per for j in range(per)]
+
+    def add(k, total):
+        a_copy(k).wait_recv()
+        return total + a_rcv[k].astype(F32)
+
+    b_buf[quad] = lax.fori_loop(1, members, add, a_src[mine].astype(F32)).astype(BF16)
 
     def b_copy(j):
-        away = lax.rem(owners[j] - seq + S, S)
+        there = lax.rem(quad + j, quads)
         return remote(
-            b_src.at[j], b_rcv.at[away], b_send.at[j], b_recv.at[away], {"seq": jnp.int32(owners[j])}
-        )
-
-    mine = jnp.int32(0)
-    owner = seq == owners[0]
-    for j in range(1, per):
-        mine = jnp.where(seq == owners[j], j, mine)
-        owner = owner | (seq == owners[j])
-
-    for j in range(per):
-        @pl.when(seq != owners[j])
-        def _():
-            b_copy(j).start()
-
-    def c_copy(k):
+            b_buf.at[quad], b_buf.at[quad], b_send.at[j], b_recv.at[quad],
+            {"seq": there * QUAD + place},
+        )
+
+    def b_from(j):
+        there = lax.rem(quad + j, quads)
         return remote(
-            c_buf.at[mine], c_buf.at[mine], c_send.at[k], c_recv.at[mine], {"seq": lax.rem(seq + k, S)}
-        )
-
-    @pl.when(owner)
-    def _():
-        total = b_src[mine].astype(F32)
-        for k in range(1, S):
-            remote(
-                b_src.at[0], b_rcv.at[k], b_send.at[0], b_recv.at[k], {"seq": lax.rem(seq + k, S)}
-            ).wait_recv()
-            total = total + b_rcv[k].astype(F32)
-        c_buf[mine] = total.astype(BF16)
-        for k in range(1, S):
-            c_copy(k).start()
-
-    for j in range(per):
-        @pl.when(seq != owners[j])
-        def _():
-            remote(
-                b_src.at[j], c_buf.at[j], c_send.at[0], c_recv.at[j], {"seq": jnp.int32(owners[j])}
-            ).wait_recv()
+            b_buf.at[there], b_buf.at[there], b_send.at[j], b_recv.at[there],
+            {"seq": there * QUAD + place},
+        )
+
+    send([b_copy(j) for j in range(1, quads)])
+    for j in range(1, quads):
+        b_from(j).wait_recv()
+    total = b_buf[0].astype(F32)
+    for j in range(1, quads):
+        total = total + b_buf[j].astype(F32)
+    c_buf[...] = total.astype(BF16)
 
     def d_copy(k):
-        return remote(
-            c_buf, d_buf.at[dp], d_send.at[k], d_recv.at[dp], {"dp": lax.rem(dp + k, D)}
-        )
-
-    send([d_copy(k) for k in range(1, D)])
+        where = member(k)[1]
+        return remote(c_buf, d_buf.at[mine], d_send.at[k], d_recv.at[mine], where)
 
     def d_from(k):
-        peer = lax.rem(dp + k, D)
-        return remote(c_buf, d_buf.at[peer], d_send.at[k], d_recv.at[peer], {"dp": peer})
-
-    coming["d"] = [d_from(k) for k in range(1, D)]
-    d_buf[dp] = c_buf[...]
+        piece, where = member(k)
+        return remote(c_buf, d_buf.at[piece], d_send.at[k], d_recv.at[piece], where)
+
+    each(1, members, lambda k: d_copy(k).start())
+    d_buf[mine] = c_buf[...]
 
     gp = gpt.T
     arrive("dv")
@@ -449,17 +448,14 @@
             total = total + dot_general(dv_buf[k], wfull[k, h, row : row + width, :], NT)
         dn_ref[:, at] = total.astype(BF16)
 
-    arrive("d")
+    each(1, members, lambda k: d_from(k).wait_recv())
     factor = 2.0 / math.sqrt(D * S * B)
     for i in range(rank // 16):
-        for j in range(across):
-            p, q = tile_at(i, j)
-            value = d_buf[p, q].astype(F32) * factor
-            if j < feats // 128:
-                ga_ref[i * 16 : i * 16 + 16, j * 128 : j * 128 + 128] = value
-            else:
-                c = j * 128 - feats
-                gb_ref[i * 16 : i * 16 + 16, c : c + 128] = value
+        at = slice(i * 16, i * 16 + 16)
+        for j in range(wide_a):
+            ga_ref[at, j * 128 : j * 128 + 128] = d_buf[tile_a(i, j)].astype(F32) * factor
+        for j in range(wide_b):
+            gb_ref[at, j * 128 : j * 128 + 128] = d_buf[tile_b(i, j)].astype(F32) * factor
 
     for c in sent:
         c.wait_send()
@@ -472,15 +468,8 @@
         @pl.when(runs(b))
         def _(b=b):
             up_to(a, b).wait_send()
-    for j in range(per):
-        @pl.when(seq != owners[j])
-        def _():
-            b_copy(j).wait_send()
-
-    @pl.when(owner)
-    def _():
-        for k in range(1, S):
-            c_copy(k).wait_send()
+    each(1, members, lambda k: a_copy(k).wait_send())
+    each(1, members, lambda k: d_copy(k).wait_send())
 
 
 def body(
@@ -493,7 +482,8 @@
     pairs = heads // 2
     feats = normed.shape[2]
     rank, cols = adapter_up.shape
-    per = (rank // 16) * ((feats + cols) // 128) // D
+    members = D * QUAD
+    per = -(-(rank // 16) * ((feats + cols) // 128) // members)
     hbm = pl.BlockSpec(memory_space=pltpu.HBM)
     vmem = pl.BlockSpec(memory_space=pltpu.VMEM)
     dma = pltpu.SemaphoreType.DMA
@@ -530,12 +520,12 @@
             pltpu.VMEM((T, rank, B), BF16),
             pltpu.VMEM((T, rank, B), BF16),
             pltpu.VMEM((T, B, cols), BF16),
-            pltpu.VMEM((D, per, 16, 128), BF16),
-            pltpu.VMEM((D, per, 16, 128), BF16),
+            pltpu.VMEM((members, per, 16, 128), BF16),
+            pltpu.VMEM((members, per, 16, 128), BF16),
+            pltpu.VMEM((S // QUAD, per, 16, 128), BF16),
             pltpu.VMEM((per, 16, 128), BF16),
-            pltpu.VMEM((S, 16, 128), BF16),
-            pltpu.VMEM((per, 16, 128), BF16),
-            pltpu.VMEM((D, per, 16, 128), BF16),
+            pltpu.VMEM((members, per, 16, 128), BF16),
+            pltpu.SemaphoreType.REGULAR,
             dma((9 + heads,)),
             dma((S,)),
             dma((S,)),
@@ -551,14 +541,12 @@
             dma((T,)),
             dma((T,)),
             dma((T,)),
-            dma((D,)),
-            dma((D,)),
-            dma((per,)),
-            dma((S,)),
-            dma((S,)),
-            dma((per,)),
-            dma((D,)),
-            dma((D,)),
+            dma((members,)),
+            dma((members,)),
+            dma((S // QUAD,)),
+            dma((S // QUAD,)),
+            dma((members,)),
+            dma((members,)),
         ],
         compiler_params=pltpu.CompilerParams(
             collective_id=0, has_side_effects=True, vmem_limit_bytes=40 * 1024 * 1024

time: 88.5 us -> 90.9 us (1.027)
  Pallas kernels: 85.7 us -> 88.2 us
    pallas_call x1, Pallas kernels: 85.7 us -> 88.2 us  [body(): pl.pallas_call(functools.partial(kernel, shape), out_shape=(jax.ShapeDtyp...]
where the time goes in v4:
time: 90.9 us; the launch traced here: 90.8 us
  Pallas kernels  88.2 us (97%)
  local copies, waits for them, and re-layouts  2.04 us (2%)
    pallas_call x1, Pallas kernels, body(): pl.pallas_call(functools.partial(kernel, shape), out_shape=(jax.ShapeDtyp...  88.2 us
    unnamed x3, local copies, waits for them, and re-layouts  2.04 us

profile of v4, /device:TPU:1, one launch (start us, length us, event | category | flops | bytes accessed | tf_op | source)
XLA Modules:
  0.0 90.8 jit_solution(5979387461454732988)
XLA Ops:
  0.6 88.2 %value_backward.1 = (bf16[128,1024]{1,0:T(8,128)(2,1)S(1)}, f32[64,1024]{1,0:T(8,128)S(1)}, f32[64,256]{1,0:T(8,128)S(1)}) custom-call(bf16[128,2048]{1,0:T(8,128)(2,1)} %bitcast.9, bf16[128,256]{1,0:T(8,128)(2,1)} %bitcast.13, bf16[128,2048]{1,0:T(8,128)(2,1)} %bitcast.10, bf16[128,1024]{1,0:T(8,128)(2,1)} %bitcast.11, s32[1,8]{1,0:T(1,128)} %len_hbm.1, ...), custom_call_target="tpu_custom_call" | custom-call | tf_op jit(solution)/shard_map/value_backward/pallas_call | solution.py:490
  88.8 0.7 copy.15
  89.5 0.7 copy.16
  90.2 0.6 copy.17

commit v5 on v4

--- a/solution.py
+++ b/solution.py
@@ -31,22 +31,22 @@
 class Tree:
     def __init__(self, size):
         if size == 16:
-            self.parent = {3: 0, 1: 0, 13: 0, 6: 3, 2: 3, 11: 13, 12: 13, 10: 11, 9: 11}
+            self.parent = {3: 0, 1: 0, 11: 0, 6: 3, 2: 3, 12: 11, 10: 11, 9: 11}
             self.parent.update({8: 6, 4: 6, 7: 6, 5: 6})
-            self.after = {3: [], 13: [3, 1], 11: [11, 2], 6: [6]}
+            self.after = {3: [], 11: [3, 1, 11], 6: [2, 6]}
             self.final = [12, 10, 9, 7, 5, 8, 4]
-            self.up = [8, 4, 7, 5, 10, 9, 12, 2, 1, 6, 11, 3, 13]
-            self.passing = [13]
+            self.up = [8, 4, 7, 5, 12, 10, 9, 2, 1, 6, 11, 3]
+            self.far = 11
         else:
             self.parent = {b: b - 1 for b in range(1, size)}
             self.after = {b: [b] for b in range(1, size - 1)}
             self.final = [size - 1]
             self.up = list(range(size - 1, 0, -1))
-            self.passing = []
+            self.far = None
         self.near = [k for k in (1, 2, 3) if 2 * k <= size]
         self.relays = list(self.after)
         self.children = {a: [b for b in self.parent if self.parent[b] == a] for a in range(size)}
-        self.least = {b: min(x for x in self.below(b) if x not in self.passing) for b in self.parent}
+        self.least = {b: min(self.below(b)) for b in self.parent}
 
     def below(self, b):
         return [b] + [x for child in self.children[b] for x in self.below(child)]
@@ -146,6 +146,15 @@
     greet("tensor", ten, T)
     greet("dp", dp, D)
     greeted = 2 * len(tree.near) + T + D - 2
+    if tree.far:
+        owner_there = lax.rem(seq - tree.far + S, S)
+
+        @pl.when(owner_there + tree.least[tree.far] <= last)
+        def _():
+            pl.semaphore_signal(barrier, inc=1, device_id={"seq": owner_there}, device_id_type=MESH)
+
+        greeted = greeted + (seq + tree.least[tree.far] <= last).astype(jnp.int32)
+
     def k_copy(a, b, where):
         return remote(kbuf.at[a], kbuf.at[b], k_send.at[b], k_recv.at[b], {"seq": where})
 
@@ -291,8 +300,6 @@
     def gather(a, keep):
         if a == 0:
             partial(0)
-        elif a in tree.passing:
-            acc_ref[...] = jnp.zeros(acc_ref.shape, F32)
         else:
             @pl.when(seq >= a)
             def _():
@@ -360,8 +367,12 @@
         n = (rank // 16) * wide_a + i * wide_b + j
         return n % members, n // members
 
-    for n in range(n_tiles, members * a_src.shape[1]):
-        a_src[n % members, n // members] = jnp.zeros((16, 128), BF16)
+    per = a_src.shape[1]
+    full = n_tiles // members
+
+    def has(piece, slot):
+        return slot * members + piece < n_tiles
+
     part_b = dot(xat, dv)
     for i in range(rank // 16):
         for j in range(cols // 128):
@@ -383,25 +394,52 @@
         at = lax.rem(place + lax.rem(k, QUAD), QUAD)
         return there * QUAD + at, {"dp": there, "seq": quad * QUAD + at}
 
-    def a_copy(k):
+    def a_copy(k, slot):
         piece, where = member(k)
-        return remote(a_src.at[piece], a_rcv.at[k], a_send.at[k], a_recv.at[k], where)
-
-    def each(first, end, act):
+        return remote(
+            a_src.at[piece, slot], a_rcv.at[k, slot], a_send.at[k, slot], a_recv.at[k, slot], where
+        )
+
+    def each(act):
         def one(k, carry):
             act(k)
             return carry
-        lax.fori_loop(first, end, one, 0)
-
+        lax.fori_loop(1, members, one, 0)
+
+    far_first = [
+        d * QUAD + z
+        for d in sorted(range(D), key=lambda d: -min(d, D - d))
+        for z in reversed(range(QUAD))
+        if d + z
+    ]
     pl.semaphore_wait(met_sem, D - 1)
-    each(1, members, lambda k: a_copy(k).start())
+    for k in far_first:
+        for slot in range(full):
+            a_copy(k, slot).start()
+    for slot in range(full, per):
+        @each
+        def _(k, slot=slot):
+            @pl.when(has(member(k)[0], slot))
+            def _():
+                a_copy(k, slot).start()
     own_weights()
 
-    def add(k, total):
-        a_copy(k).wait_recv()
-        return total + a_rcv[k].astype(F32)
-
-    b_buf[quad] = lax.fori_loop(1, members, add, a_src[mine].astype(F32)).astype(BF16)
+    def summed(slot):
+        def add(k, total):
+            a_copy(k, slot).wait_recv()
+            return total + a_rcv[k, slot].astype(F32)
+        total = lax.fori_loop(1, members, add, a_src[mine, slot].astype(F32))
+        b_buf[quad, slot] = total.astype(BF16)
+
+    for slot in range(per):
+        if slot < full:
+            summed(slot)
+        else:
+            b_buf[quad, slot] = jnp.zeros((16, 128), BF16)
+
+            @pl.when(has(mine, slot))
+            def _(slot=slot):
+                summed(slot)
 
     def b_copy(j):
         there = lax.rem(quad + j, quads)
@@ -425,15 +463,25 @@
         total = total + b_buf[j].astype(F32)
     c_buf[...] = total.astype(BF16)
 
-    def d_copy(k):
+    def d_copy(k, slot):
         where = member(k)[1]
-        return remote(c_buf, d_buf.at[mine], d_send.at[k], d_recv.at[mine], where)
-
-    def d_from(k):
+        return remote(
+            c_buf.at[slot], d_buf.at[mine, slot], d_send.at[k, slot], d_recv.at[mine, slot], where
+        )
+
+    def d_from(k, slot):
         piece, where = member(k)
-        return remote(c_buf, d_buf.at[piece], d_send.at[k], d_recv.at[piece], where)
-
-    each(1, members, lambda k: d_copy(k).start())
+        return remote(
+            c_buf.at[slot], d_buf.at[piece, slot], d_send.at[k, slot], d_recv.at[piece, slot], where
+        )
+
+    for k in far_first:
+        for slot in range(full):
+            d_copy(k, slot).start()
+    for slot in range(full, per):
+        @pl.when(has(mine, slot))
+        def _(slot=slot):
+            each(lambda k: d_copy(k, slot).start())
     d_buf[mine] = c_buf[...]
 
     gp = gpt.T
@@ -448,7 +496,12 @@
             total = total + dot_general(dv_buf[k], wfull[k, h, row : row + width, :], NT)
         dn_ref[:, at] = total.astype(BF16)
 
-    each(1, members, lambda k: d_from(k).wait_recv())
+    for slot in range(per):
+        @each
+        def _(k, slot=slot):
+            @pl.when(has(member(k)[0], slot))
+            def _():
+                d_from(k, slot).wait_recv()
     factor = 2.0 / math.sqrt(D * S * B)
     for i in range(rank // 16):
         at = slice(i * 16, i * 16 + 16)
@@ -468,8 +521,16 @@
         @pl.when(runs(b))
         def _(b=b):
             up_to(a, b).wait_send()
-    each(1, members, lambda k: a_copy(k).wait_send())
-    each(1, members, lambda k: d_copy(k).wait_send())
+    for slot in range(per):
+        @each
+        def _(k, slot=slot):
+            @pl.when(has(member(k)[0], slot))
+            def _():
+                a_copy(k, slot).wait_send()
+
+            @pl.when(has(mine, slot))
+            def _():
+                d_copy(k, slot).wait_send()
 
 
 def body(
@@ -541,12 +602,12 @@
             dma((T,)),
             dma((T,)),
             dma((T,)),
-            dma((members,)),
-            dma((members,)),
+            dma((members, per)),
+            dma((members, per)),
             dma((S // QUAD,)),
             dma((S // QUAD,)),
-            dma((members,)),
-            dma((members,)),
+            dma((members, per)),
+            dma((members, per)),
         ],
         compiler_params=pltpu.CompilerParams(
             collective_id=0, has_side_effects=True, vmem_limit_bytes=40 * 1024 * 1024

time: 90.9 us -> 87.2 us (0.959)
  Pallas kernels: 88.2 us -> 84.4 us
    pallas_call x1, Pallas kernels: 88.2 us -> 84.4 us  [body(): pl.pallas_call(functools.partial(kernel, shape), out_shape=(jax.ShapeDtyp...]
where the time goes in v5:
time: 87.2 us; the launch traced here: 87.1 us
  Pallas kernels  84.4 us (97%)
  local copies, waits for them, and re-layouts  2.04 us (2%)
    pallas_call x1, Pallas kernels, body(): pl.pallas_call(functools.partial(kernel, shape), out_shape=(jax.ShapeDtyp...  84.4 us
    unnamed x3, local copies, waits for them, and re-layouts  2.04 us

profile of v5, /device:TPU:1, one launch (start us, length us, event | category | flops | bytes accessed | tf_op | source)
XLA Modules:
  0.0 87.1 jit_solution(8694561514315305593)
XLA Ops:
  0.6 84.4 %value_backward.1 = (bf16[128,1024]{1,0:T(8,128)(2,1)S(1)}, f32[64,1024]{1,0:T(8,128)S(1)}, f32[64,256]{1,0:T(8,128)S(1)}) custom-call(bf16[128,2048]{1,0:T(8,128)(2,1)} %bitcast.9, bf16[128,256]{1,0:T(8,128)(2,1)} %bitcast.13, bf16[128,2048]{1,0:T(8,128)(2,1)} %bitcast.10, bf16[128,1024]{1,0:T(8,128)(2,1)} %bitcast.11, s32[1,8]{1,0:T(1,128)} %len_hbm.1, ...), custom_call_target="tpu_custom_call" | custom-call | tf_op jit(solution)/shard_map/value_backward/pallas_call | solution.py:551
  85.0 0.7 copy.15
  85.7 0.7 copy.16
  86.4 0.6 copy.17

commit v6 on v5

--- a/solution.py
+++ b/solution.py
@@ -155,20 +155,23 @@
 
         greeted = greeted + (seq + tree.least[tree.far] <= last).astype(jnp.int32)
 
-    def k_copy(a, b, where):
-        return remote(kbuf.at[a], kbuf.at[b], k_send.at[b], k_recv.at[b], {"seq": where})
+    def k_copy(a, b, g, where):
+        return remote(
+            kbuf.at[a, g], kbuf.at[b, g], k_send.at[b, g], k_recv.at[b, g], {"seq": where}
+        )
 
     def runs(b):
         return lax.rem(seq - b + S, S) + tree.least[b] <= last
 
-    def pass_down(a):
+    def pass_down(a, g):
         for b in tree.children[a]:
             @pl.when(lax.rem(seq - a + S, S) + tree.least[b] <= last)
             def _(b=b):
-                k_copy(a, b, lax.rem(seq + b - a + S, S)).start()
+                k_copy(a, b, g, lax.rem(seq + b - a + S, S)).start()
 
     def k_arrive(b):
-        k_copy(0, b, seq).wait_recv()
+        for g in range(KV):
+            k_copy(0, b, g, seq).wait_recv()
 
     ready("q")
     ready("k")
@@ -210,7 +213,8 @@
 
     attend(0)
     pl.semaphore_wait(barrier, greeted)
-    pass_down(0)
+    for g in range(KV):
+        pass_down(0, g)
     for k in range(1, D):
         pl.semaphore_signal(
             met_sem, inc=1, device_id={"dp": lax.rem(dp + k, D)}, device_id_type=MESH
@@ -260,8 +264,9 @@
     for n, a in enumerate(tree.relays):
         @pl.when(runs(a))
         def _(a=a):
-            k_arrive(a)
-            pass_down(a)
+            for g in range(KV):
+                k_copy(0, a, g, seq).wait_recv()
+                pass_down(a, g)
         if n + 1 < T:
             send_weights(n + 1)
         for b in tree.after[a]:
@@ -280,47 +285,48 @@
     l_ref[...] = 1.0 / l_ref[...]
     ready("g")
 
-    def partial(slot):
-        for g in range(KV):
-            total = None
-            for i in range(per_kv):
-                hp = g * per_kv + i
-                factor = jnp.exp2(ms_ref[slot, hp] - m_ref[hp]) * l_ref[hp]
-                p = (w_ref[slot, hp].astype(F32) * factor).astype(BF16)
-                one = dot(p, gv[hp])
-                total = one if total is None else total + one
-            acc_ref[g] = total
-
-    def s_copy(a, b, where):
-        return remote(rs_out.at[b], rs_in.at[b], s_send.at[b], s_recv.at[b], {"seq": where})
-
-    def up_to(a, b):
-        return s_copy(a, b, lax.rem(seq + a - b + S, S))
-
-    def gather(a, keep):
+    def partial(slot, g):
+        total = None
+        for i in range(per_kv):
+            hp = g * per_kv + i
+            factor = jnp.exp2(ms_ref[slot, hp] - m_ref[hp]) * l_ref[hp]
+            p = (w_ref[slot, hp].astype(F32) * factor).astype(BF16)
+            one = dot(p, gv[hp])
+            total = one if total is None else total + one
+        acc_ref[g] = total
+
+    def s_copy(b, g, where):
+        return remote(
+            rs_out.at[b, g], rs_in.at[b, g], s_send.at[b, g], s_recv.at[b, g], {"seq": where}
+        )
+
+    def up_from(b, g):
+        return s_copy(b, g, lax.rem(seq + tree.parent[b] - b + S, S))
+
+    def gather(a, g):
         if a == 0:
-            partial(0)
+            partial(0, g)
         else:
             @pl.when(seq >= a)
             def _():
-                partial(a)
+                partial(a, g)
 
             @pl.when(seq < a)
             def _():
-                acc_ref[...] = jnp.zeros(acc_ref.shape, F32)
+                acc_ref[g] = jnp.zeros((B, HEAD), F32)
         for b in tree.children[a]:
             @pl.when(lax.rem(seq - a + S, S) + tree.least[b] <= last)
             def _(b=b):
-                s_copy(a, b, seq).wait_recv()
-                acc_ref[...] += rs_in[b].astype(F32)
-        if keep:
-            rs_out[a] = acc_ref[...].astype(BF16)
+                s_copy(b, g, seq).wait_recv()
+                acc_ref[g] += rs_in[b, g].astype(F32)
 
     for b in tree.up:
         @pl.when(runs(b))
         def _(b=b):
-            gather(b, True)
-            up_to(tree.parent[b], b).start()
+            for g in range(KV):
+                gather(b, g)
+                rs_out[b, g] = acc_ref[g].astype(BF16)
+                up_from(b, g).start()
 
     arrive("xa")
     xat = xa_buf[0].astype(F32)
@@ -331,8 +337,8 @@
     send([wc_copy(k, core) for k in range(1, T)])
     coming["wc"] = [wc_copy(k, 1 - core) for k in range(1, T)]
     ready("up")
-    gather(0, False)
     for g in range(KV):
+        gather(0, g)
         dv_buf[0, :, g * HEAD : (g + 1) * HEAD] = acc_ref[g].astype(BF16)
 
     dv = dv_buf[0]
@@ -456,33 +462,6 @@
         )
 
     send([b_copy(j) for j in range(1, quads)])
-    for j in range(1, quads):
-        b_from(j).wait_recv()
-    total = b_buf[0].astype(F32)
-    for j in range(1, quads):
-        total = total + b_buf[j].astype(F32)
-    c_buf[...] = total.astype(BF16)
-
-    def d_copy(k, slot):
-        where = member(k)[1]
-        return remote(
-            c_buf.at[slot], d_buf.at[mine, slot], d_send.at[k, slot], d_recv.at[mine, slot], where
-        )
-
-    def d_from(k, slot):
-        piece, where = member(k)
-        return remote(
-            c_buf.at[slot], d_buf.at[piece, slot], d_send.at[k, slot], d_recv.at[piece, slot], where
-        )
-
-    for k in far_first:
-        for slot in range(full):
-            d_copy(k, slot).start()
-    for slot in range(full, per):
-        @pl.when(has(mine, slot))
-        def _(slot=slot):
-            each(lambda k: d_copy(k, slot).start())
-    d_buf[mine] = c_buf[...]
 
     gp = gpt.T
     arrive("dv")
@@ -495,6 +474,35 @@
         for k in range(T):
             total = total + dot_general(dv_buf[k], wfull[k, h, row : row + width, :], NT)
         dn_ref[:, at] = total.astype(BF16)
+
+
+    for j in range(1, quads):
+        b_from(j).wait_recv()
+    sums = b_buf[0].astype(F32)
+    for j in range(1, quads):
+        sums = sums + b_buf[j].astype(F32)
+    c_buf[...] = sums.astype(BF16)
+
+    def d_copy(k, slot):
+        where = member(k)[1]
+        return remote(
+            c_buf.at[slot], d_buf.at[mine, slot], d_send.at[k, slot], d_recv.at[mine, slot], where
+        )
+
+    def d_from(k, slot):
+        piece, where = member(k)
+        return remote(
+            c_buf.at[slot], d_buf.at[piece, slot], d_send.at[k, slot], d_recv.at[piece, slot], where
+        )
+
+    for k in far_first:
+        for slot in range(full):
+            d_copy(k, slot).start()
+    for slot in range(full, per):
+        @pl.when(has(mine, slot))
+        def _(slot=slot):
+            each(lambda k: d_copy(k, slot).start())
+    d_buf[mine] = c_buf[...]
 
     for slot in range(per):
         @each
@@ -516,11 +524,13 @@
 
         @pl.when(lax.rem(seq - a + S, S) + tree.least[b] <= last)
         def _(a=a, b=b):
-            k_copy(a, b, seq).wait_send()
+            for g in range(KV):
+                k_copy(a, b, g, seq).wait_send()
 
         @pl.when(runs(b))
         def _(b=b):
-            up_to(a, b).wait_send()
+            for g in range(KV):
+                up_from(b, g).wait_send()
     for slot in range(per):
         @each
         def _(k, slot=slot):
@@ -588,10 +598,10 @@
             pltpu.VMEM((members, per, 16, 128), BF16),
             pltpu.SemaphoreType.REGULAR,
             dma((9 + heads,)),
-            dma((S,)),
-            dma((S,)),
-            dma((S,)),
-            dma((S,)),
+            dma((S, KV)),
+            dma((S, KV)),
+            dma((S, KV)),
+            dma((S, KV)),
             dma((T,)),
             dma((T,)),
             dma((T,)),

time: 87.2 us -> 88.5 us (1.015)
  Pallas kernels: 84.4 us -> 85.7 us
    pallas_call x1, Pallas kernels: 84.4 us -> 85.7 us  [body(): pl.pallas_call(functools.partial(kernel, shape), out_shape=(jax.ShapeDtyp...]
where the time goes in v6:
time: 88.5 us; the launch traced here: 88.4 us
  Pallas kernels  85.7 us (97%)
  local copies, waits for them, and re-layouts  2.04 us (2%)
    pallas_call x1, Pallas kernels, body(): pl.pallas_call(functools.partial(kernel, shape), out_shape=(jax.ShapeDtyp...  85.7 us
    unnamed x3, local copies, waits for them, and re-layouts  2.04 us

profile of v6, /device:TPU:1, one launch (start us, length us, event | category | flops | bytes accessed | tf_op | source)
XLA Modules:
  0.0 88.4 jit_solution(61546643384956133)
XLA Ops:
  0.6 85.7 %value_backward.1 = (bf16[128,1024]{1,0:T(8,128)(2,1)S(1)}, f32[64,1024]{1,0:T(8,128)S(1)}, f32[64,256]{1,0:T(8,128)S(1)}) custom-call(bf16[128,2048]{1,0:T(8,128)(2,1)} %bitcast.9, bf16[128,256]{1,0:T(8,128)(2,1)} %bitcast.13, bf16[128,2048]{1,0:T(8,128)(2,1)} %bitcast.10, bf16[128,1024]{1,0:T(8,128)(2,1)} %bitcast.11, s32[1,8]{1,0:T(1,128)} %len_hbm.1, ...), custom_call_target="tpu_custom_call" | custom-call | tf_op jit(solution)/shard_map/value_backward/pallas_call | solution.py:561
  86.4 0.7 copy.15
  87.1 0.7 copy.16
  87.8 0.6 copy.17

commit v7 on v5

--- a/solution.py
+++ b/solution.py
@@ -32,10 +32,10 @@
     def __init__(self, size):
         if size == 16:
             self.parent = {3: 0, 1: 0, 11: 0, 6: 3, 2: 3, 12: 11, 10: 11, 9: 11}
-            self.parent.update({8: 6, 4: 6, 7: 6, 5: 6})
+            self.parent.update({4: 3, 8: 6, 7: 6, 5: 6})
             self.after = {3: [], 11: [3, 1, 11], 6: [2, 6]}
-            self.final = [12, 10, 9, 7, 5, 8, 4]
-            self.up = [8, 4, 7, 5, 12, 10, 9, 2, 1, 6, 11, 3]
+            self.final = [4, 12, 10, 9, 7, 5, 8]
+            self.up = [8, 7, 5, 4, 12, 10, 9, 2, 1, 6, 11, 3]
             self.far = 11
         else:
             self.parent = {b: b - 1 for b in range(1, size)}

time: 87.2 us -> 91.5 us (1.049)
  Pallas kernels: 84.4 us -> 88.7 us
    pallas_call x1, Pallas kernels: 84.4 us -> 88.7 us  [body(): pl.pallas_call(functools.partial(kernel, shape), out_shape=(jax.ShapeDtyp...]
where the time goes in v7:
time: 91.5 us; the launch traced here: 91.4 us
  Pallas kernels  88.7 us (97%)
  local copies, waits for them, and re-layouts  2.04 us (2%)
    pallas_call x1, Pallas kernels, body(): pl.pallas_call(functools.partial(kernel, shape), out_shape=(jax.ShapeDtyp...  88.7 us
    unnamed x3, local copies, waits for them, and re-layouts  2.04 us

profile of v7, /device:TPU:1, one launch (start us, length us, event | category | flops | bytes accessed | tf_op | source)
XLA Modules:
  0.0 91.4 jit_solution(10192515644197137252)
XLA Ops:
  0.6 88.7 %value_backward.1 = (bf16[128,1024]{1,0:T(8,128)(2,1)S(1)}, f32[64,1024]{1,0:T(8,128)S(1)}, f32[64,256]{1,0:T(8,128)S(1)}) custom-call(bf16[128,2048]{1,0:T(8,128)(2,1)} %bitcast.9, bf16[128,256]{1,0:T(8,128)(2,1)} %bitcast.13, bf16[128,2048]{1,0:T(8,128)(2,1)} %bitcast.10, bf16[128,1024]{1,0:T(8,128)(2,1)} %bitcast.11, s32[1,8]{1,0:T(1,128)} %len_hbm.1, ...), custom_call_target="tpu_custom_call" | custom-call | tf_op jit(solution)/shard_map/value_backward/pallas_call | solution.py:551
  89.3 0.7 copy.15
  90.0 0.7 copy.16
  90.8 0.6 copy.17
